TPU v7x, 128 devices: a whole 4x4x4 slice. The times are simulated.
128 devices in a mesh: tm: 8 (over x_hi, y), space: 16 (over z, x_lo, core).
Axes of the slice: x: 4 (x_hi: 2, x_lo: 2; x = x_hi * 2 + x_lo), y: 4, z: 4, core: 2. Of those that a mesh axis runs over, the one named last changes fastest.
Arguments:
- forcing: float32 [8, 128, 16384], P('tm', 'space'), may hold values from -6 to 6
- conductivity: float32 [128, 16384], P('space'), may hold values from 0.1 to 1
Outputs:
- solution: float32 [8, 128, 16384], P('tm', 'space')
All inputs are finite; a program needn't handle non-finite values.
Results may differ from a plain program's by a relative error of at most 0.0001.
Values sent between devices are 32-bit elements; how exact they have to be, the bound alone decides.
No kernel may reach another device: no remote copies, remote signals or barrier semaphores. Data moves between devices by JAX's collectives and lax.ppermute only.
A program may use at most 64 MiB of HBM per device.

v0:
```python
import jax
import jax.numpy as jnp
from jax import lax
from jax.sharding import PartitionSpec as P

ITERS = 3


def padded_2(x, sides, width):
    for axis, dim in sides:
        peers, length = (lax.axis_size(axis), x.shape[dim])
        up = [(i, (i + 1) % peers) for i in range(peers - 1)]
        down = [(j, i) for i, j in up]
        last = lax.slice_in_dim(x, length - width, length, axis=dim)
        leading = lax.slice_in_dim(x, 0, width, axis=dim)
        before = lax.ppermute(last, axis, up)
        after = lax.ppermute(leading, axis, down)
        x = jnp.concatenate([before, x, after], axis=dim)
    return x


def passed_along(block, axis, distance):
    devices = range(lax.axis_size(axis))
    route = [(i - distance, i) for i in devices if i - distance in devices]
    return lax.ppermute(block, axis, route)


def edge_weights(kpad):
    center = kpad[1:-1, 1:-1]
    north = 0.5 * (center + kpad[:-2, 1:-1])
    south = 0.5 * (center + kpad[2:, 1:-1])
    west = 0.5 * (center + kpad[1:-1, :-2])
    east = 0.5 * (center + kpad[1:-1, 2:])
    diag = 1.0 + north + south + west + east
    return (north, south, west, east, diag)


def neighbours(extended, north, south, west, east):
    padded = jnp.pad(extended, ((0, 0), (0, 0), (1, 1)))
    total = north * padded[:, :-2, 1:-1] + south * padded[:, 2:, 1:-1]
    return total + west * padded[:, 1:-1, :-2] + east * padded[:, 1:-1, 2:]


def level(array, depth):
    cut = 3 - depth
    return array[cut : array.shape[0] - cut]


def turn_back(received):
    reversed_pieces = received[:, ::-1]
    return lax.all_to_all(reversed_pieces, "tm", split_axis=1, concat_axis=1, tiled=True)


def mirror(field):
    steps, rows, columns = field.shape
    count = lax.axis_size("tm")
    pieces = field.reshape(steps, count, rows // count, columns)
    moved = turn_back(lax.all_to_all(pieces, "tm", split_axis=1, concat_axis=1, tiled=True))
    return moved.reshape(steps, rows, columns)[::-1]


def body(forcing, conductivity):
    kext = padded_2(conductivity, (("space", 0),), 4)
    north3, south3, west3, east3, diag3 = edge_weights(jnp.pad(kext, ((0, 0), (1, 1))))
    scale3 = 1.0 / jnp.sqrt(diag3)
    north, south, west, east, diag = [level(a, 0) for a in (north3, south3, west3, east3, diag3)]
    scale = level(scale3, 0)

    def precondition(field):

        def apply_step(term):
            inner = padded_2(scale * term, (("space", 1),), 1)
            return scale * neighbours(inner, north, south, west, east)

        first = scale * field
        second = apply_step(first)
        third = 2.0 * apply_step(second) - first
        fourth = 2.0 * apply_step(third) - second
        return scale * (first + 0.5 * second + 0.25 * third + 0.125 * fourth)

    vec = mirror(forcing)
    vec_old = jnp.zeros_like(vec)
    zvec = precondition(vec)
    gamma = jnp.sqrt(lax.psum(jnp.sum(zvec * vec), ("tm", "space")))
    gamma_old = jnp.float32(1.0)
    wvec = jnp.zeros_like(vec)
    wvec_old = jnp.zeros_like(vec)
    solution = jnp.zeros_like(vec)
    cos_now = jnp.float32(1.0)
    cos_old = jnp.float32(1.0)
    sin_now = jnp.float32(0.0)
    sin_old = jnp.float32(0.0)
    eta = gamma
    for step in range(ITERS):
        zvec = zvec / gamma
        extended = padded_2(zvec, (("space", 1),), 1)
        stepped = diag * zvec - neighbours(extended, north, south, west, east)
        prior = passed_along(zvec, "tm", 1)
        earlier = jnp.concatenate([prior, zvec[:-1]], 0)
        image = mirror(stepped - earlier)
        delta = lax.psum(jnp.sum(image * zvec), ("tm", "space"))
        vec_new = image - delta / gamma * vec - gamma / gamma_old * vec_old
        zvec_new = precondition(vec_new)
        gamma_new = jnp.sqrt(lax.psum(jnp.sum(zvec_new * vec_new), ("tm", "space")))
        vec_old, vec = (vec, vec_new)
        alpha_zero = cos_now * delta - cos_old * sin_now * gamma
        alpha_one = jnp.sqrt(alpha_zero * alpha_zero + gamma_new * gamma_new)
        alpha_two = sin_now * delta + cos_old * cos_now * gamma
        alpha_three = sin_old * gamma
        cos_new = alpha_zero / alpha_one
        sin_new = gamma_new / alpha_one
        wvec_new = (zvec - alpha_three * wvec_old - alpha_two * wvec) / alpha_one
        solution = solution + cos_new * eta * wvec_new
        eta = -sin_new * eta
        zvec = zvec_new
        gamma_old, gamma = (gamma, gamma_new)
        wvec_old, wvec = (wvec, wvec_new)
        cos_old, cos_now, sin_old, sin_now = (cos_now, cos_new, sin_now, sin_new)
    return solution


def solution(mesh):
    return jax.shard_map(
        body,
        mesh=mesh,
        in_specs=(P("tm", "space", None), P("space", None)),
        out_specs=P("tm", "space", None),
        check_vma=False,
    )
```

profile of v0, /device:TPU:1, one launch (start us, length us, event | category | flops | bytes accessed | tf_op | source)
XLA Modules:
  0.0 852.9 jit_solution(13346027972024381720)
XLA Ops:
  1.4 4.6 collective-permute-start
  9.1 6.4 all-to-all-start
  16.6 9.2 %all-to-all-done = f32[1,8,1,16384]{3,2,0,1:T(1,128)S(1)} async-done(((f32[1,8,1,16384]{3,2,0,1:T(1,128)}), f32[1,8,1,16384]{3,2,0,1:T(1,128)S(1)}, u32[]{:S(2)}, u32[]{:S(2)}) %all-to-all-start) | async-done | bytes 524320 | tf_op jit(solution)/shard_map/all_to_all | solution.py:58
  32.9 6.9 all-to-all-done.1
  41.0 6.2 collective-permute-start.2
  49.2 3.6 collective-permute-done.3
  78.4 4.6 fusion.101
  83.0 65.0 %psum.49 = f32[]{:T(128)} all-reduce(f32[]{:T(128)} %get-tuple-element.24), channel_id=1, replica_groups=mesh['tm'=8,'space'=16] {'tm','space'}, use_global_device_ids=true, to_apply=%region_1.2 | all-reduce | flops 1 | bytes 8 | tf_op jit(solution)/shard_map/psum | solution.py:84
  160.5 6.9 collective-permute-done.10
  170.2 18.5 %all_to_all.40 = f32[1,8,1,16384]{3,2,0,1:T(1,128)} all-to-all(f32[1,8,1,16384]{3,2,0,1:T(1,128)S(1)} %subtract_bitcast_fusion.2), channel_id=1, replica_groups=mesh['tm'=8,'space'=16] {'tm'}, dimensions={1} | all-to-all | bytes 1048576 | tf_op jit(solution)/shard_map/all_to_all | solution.py:58
  190.6 13.1 %all_to_all.41 = f32[1,8,1,16384]{3,2,0,1:T(1,128)S(1)} all-to-all(f32[1,8,1,16384]{3,2,0,1:T(1,128)} %rev.13), channel_id=1, replica_groups=mesh['tm'=8,'space'=16] {'tm'}, dimensions={1} | all-to-all | bytes 1048576 | tf_op jit(solution)/shard_map/all_to_all | solution.py:51
  206.2 65.1 %psum.50 = f32[]{:T(128)} all-reduce(f32[]{:T(128)} %fusion.99), channel_id=1, replica_groups=mesh['tm'=8,'space'=16] {'tm','space'}, use_global_device_ids=true, to_apply=%region_3.4 | all-reduce | flops 1 | bytes 8 | tf_op jit(solution)/shard_map/psum | solution.py:101
  289.1 3.8 collective-permute-done.14
  302.5 4.1 collective-permute-done.16
  308.8 5.3 multiply_reduce_fusion.1
  314.1 64.5 %psum.51 = f32[]{:T(128)} all-reduce(f32[]{:T(128)} %get-tuple-element.18), channel_id=1, replica_groups=mesh['tm'=8,'space'=16] {'tm','space'}, use_global_device_ids=true, to_apply=%region_5.6 | all-reduce | flops 1 | bytes 8 | tf_op jit(solution)/shard_map/psum | solution.py:104
  380.6 4.8 collective-permute-start.17
  393.2 6.1 collective-permute-done.19
  402.1 18.3 %all_to_all.42 = f32[1,8,1,16384]{3,2,0,1:T(1,128)} all-to-all(f32[1,8,1,16384]{3,2,0,1:T(1,128)S(1)} %subtract_bitcast_fusion.1), channel_id=1, replica_groups=mesh['tm'=8,'space'=16] {'tm'}, dimensions={1} | all-to-all | bytes 1048576 | tf_op jit(solution)/shard_map/all_to_all | solution.py:58
  422.4 14.0 %all_to_all.43 = f32[1,8,1,16384]{3,2,0,1:T(1,128)S(1)} all-to-all(f32[1,8,1,16384]{3,2,0,1:T(1,128)} %rev.14), channel_id=1, replica_groups=mesh['tm'=8,'space'=16] {'tm'}, dimensions={1} | all-to-all | bytes 1048576 | tf_op jit(solution)/shard_map/all_to_all | solution.py:51
  439.0 63.6 %psum.52 = f32[]{:T(128)} all-reduce(f32[]{:T(128)} %fusion.97), channel_id=1, replica_groups=mesh['tm'=8,'space'=16] {'tm','space'}, use_global_device_ids=true, to_apply=%region_7.8 | all-reduce | flops 1 | bytes 8 | tf_op jit(solution)/shard_map/psum | solution.py:101
  533.9 3.7 collective-permute-done.25
  539.9 6.0 multiply_reduce_fusion
  545.8 64.0 %psum.53 = f32[]{:T(128)} all-reduce(f32[]{:T(128)} %get-tuple-element.11), channel_id=1, replica_groups=mesh['tm'=8,'space'=16] {'tm','space'}, use_global_device_ids=true, to_apply=%region_9.10 | all-reduce | flops 1 | bytes 8 | tf_op jit(solution)/shard_map/psum | solution.py:104
  611.8 4.3 collective-permute-start.26
  623.9 6.5 collective-permute-done.28
  633.2 18.8 %all_to_all.44 = f32[1,8,1,16384]{3,2,0,1:T(1,128)} all-to-all(f32[1,8,1,16384]{3,2,0,1:T(1,128)S(1)} %subtract_bitcast_fusion), channel_id=1, replica_groups=mesh['tm'=8,'space'=16] {'tm'}, dimensions={1} | all-to-all | bytes 1048576 | tf_op jit(solution)/shard_map/all_to_all | solution.py:58
  653.9 13.8 %all_to_all.45 = f32[1,8,1,16384]{3,2,0,1:T(1,128)S(1)} all-to-all(f32[1,8,1,16384]{3,2,0,1:T(1,128)} %rev.15), channel_id=1, replica_groups=mesh['tm'=8,'space'=16] {'tm'}, dimensions={1} | all-to-all | bytes 1048576 | tf_op jit(solution)/shard_map/all_to_all | solution.py:51
  670.4 63.8 %psum.54 = f32[]{:T(128)} all-reduce(f32[]{:T(128)} %fusion.94), channel_id=1, replica_groups=mesh['tm'=8,'space'=16] {'tm','space'}, use_global_device_ids=true, to_apply=%region_11.12 | all-reduce | flops 1 | bytes 8 | tf_op jit(solution)/shard_map/psum | solution.py:101
  755.4 3.7 collective-permute-done.32
  777.7 6.2 fusion.105
  783.9 65.1 %psum.55 = f32[]{:T(128)} all-reduce(f32[]{:T(128)} %fusion.105), channel_id=1, replica_groups=mesh['tm'=8,'space'=16] {'tm','space'}, use_global_device_ids=true, to_apply=%region_13.14 | all-reduce | flops 1 | bytes 8 | tf_op jit(solution)/shard_map/psum | solution.py:104
  (196 shorter events, 191.7 us)
Async XLA Ops:
  1.4 14.1 %collective-permute-start = (f32[4,16384]{1,0:T(4,128)S(1)}, f32[4,16384]{1,0:T(4,128)S(1)}, u32[]{:S(2)}, u32[]{:S(2)}) collective-permute-start(f32[4,16384]{1,0:T(4,128)S(1)} %get-tuple-element.69), channel_id=1, source_target_pairs={{0,1},{1,2},{2,3},{3,4},{4,5},{5,6},{6,7},{7,8},{8,9},{9,10},{10,1... | collective-permute-start | bytes 786440 | tf_op jit(solution)/shard_map/ppermute | solution.py:16
  6.0 9.5 %collective-permute-start.1 = (f32[4,16384]{1,0:T(4,128)S(1)}, f32[4,16384]{1,0:T(4,128)}, u32[]{:S(2)}, u32[]{:S(2)}) collective-permute-start(f32[4,16384]{1,0:T(4,128)S(1)} %get-tuple-element.70), channel_id=1, source_target_pairs={{1,0},{2,1},{3,2},{4,3},{5,4},{6,5},{7,6},{8,7},{9,8},{10,9},{11,1... | collective-permute-start | bytes 786440 | tf_op jit(solution)/shard_map/ppermute | solution.py:17
  9.1 16.7 %all-to-all-start = ((f32[1,8,1,16384]{3,2,0,1:T(1,128)}), f32[1,8,1,16384]{3,2,0,1:T(1,128)S(1)}, u32[]{:S(2)}, u32[]{:S(2)}) async-start(f32[1,8,1,16384]{3,2,0,1:T(1,128)} %reshape.149), calls=%async_computation | async-start | bytes 1048576 | tf_op jit(solution)/shard_map/all_to_all | solution.py:58
  26.6 13.1 %all-to-all-start.1 = ((f32[1,8,1,16384]{3,2,0,1:T(1,128)}), f32[1,8,1,16384]{3,2,0,1:T(1,128)S(1)}, u32[]{:S(2)}, u32[]{:S(2)}) async-start(f32[1,8,1,16384]{3,2,0,1:T(1,128)} %rev.12), calls=%async_computation.1 | async-start | bytes 1048576 | tf_op jit(solution)/shard_map/all_to_all | solution.py:51
  41.0 8.2 collective-permute-start.2
  47.2 5.6 collective-permute-start.3
  55.2 4.6 collective-permute-start.4
  57.1 5.6 collective-permute-start.5
  67.8 5.0 collective-permute-start.6
  69.7 6.5 collective-permute-start.7
  149.8 7.6 collective-permute-start.8
  152.7 5.6 collective-permute-start.9
  154.6 12.8 %collective-permute-start.10 = (f32[1,8,16384]{2,0,1:T(1,128)S(1)}, f32[1,8,16384]{2,0,1:T(1,128)S(1)}, u32[]{:S(2)}, u32[]{:S(2)}) collective-permute-start(f32[1,8,16384]{2,0,1:T(1,128)S(1)} %bitcast.147), channel_id=1, source_target_pairs={{0,16},{16,32},{32,48},{48,64},{64,80},{80,96},{96,112},{1,17},{17... | collective-permute-start | bytes 1572872 | tf_op jit(solution)/shard_map/ppermute | solution.py:25
  277.2 5.6 collective-permute-start.12
  286.7 6.2 collective-permute-start.14
  300.1 6.5 collective-permute-start.16
  380.6 8.0 collective-permute-start.17
  385.3 5.6 collective-permute-start.18
  387.3 12.1 %collective-permute-start.19 = (f32[1,8,16384]{2,0,1:T(1,128)S(1)}, f32[1,8,16384]{2,0,1:T(1,128)S(1)}, u32[]{:S(2)}, u32[]{:S(2)}) collective-permute-start(f32[1,8,16384]{2,0,1:T(1,128)S(1)} %bitcast.155), channel_id=1, source_target_pairs={{0,16},{16,32},{32,48},{48,64},{64,80},{80,96},{96,112},{1,17},{17... | collective-permute-start | bytes 1572872 | tf_op jit(solution)/shard_map/ppermute | solution.py:25
  505.7 5.1 collective-permute-start.20
  508.9 5.6 collective-permute-start.21
  518.4 5.6 collective-permute-start.23
  529.1 4.9 collective-permute-start.24
  531.1 6.5 collective-permute-start.25
  611.8 7.6 collective-permute-start.26
  616.1 5.6 collective-permute-start.27
  618.0 12.4 %collective-permute-start.28 = (f32[1,8,16384]{2,0,1:T(1,128)S(1)}, f32[1,8,16384]{2,0,1:T(1,128)S(1)}, u32[]{:S(2)}, u32[]{:S(2)}) collective-permute-start(f32[1,8,16384]{2,0,1:T(1,128)S(1)} %bitcast.151), channel_id=1, source_target_pairs={{0,16},{16,32},{32,48},{48,64},{64,80},{80,96},{96,112},{1,17},{17... | collective-permute-start | bytes 1572872 | tf_op jit(solution)/shard_map/ppermute | solution.py:25
  739.8 5.6 collective-permute-start.30
  750.9 4.5 collective-permute-start.31
  752.8 6.3 collective-permute-start.32
  765.7 8.6 %collective-permute-start.33 = (f32[1,1,16384]{2,0,1:T(1,128)S(1)}, f32[1,1,16384]{2,0,1:T(1,128)S(1)}, u32[]{:S(2)}, u32[]{:S(2)}) collective-permute-start(f32[1,1,16384]{2,0,1:T(1,128)S(1)} %get-tuple-element.39), channel_id=1, source_target_pairs={{0,1},{1,2},{2,3},{3,4},{4,5},{5,6},{6,7},{7,8},{8,9},{9,10},{10,1... | collective-permute-start | bytes 196616 | tf_op jit(solution)/shard_map/ppermute | solution.py:16
  767.6 6.7 collective-permute-start.34
  (38 other events, 359.9 us)
where the time goes:
time: 863 us; the launch traced here: 853 us
  blocking collectives  548 us (63%)
  other arithmetic  103 us (12%)
  starting transfers between devices  97 us (11%)
  waiting for transfers between devices  79.2 us (9%)
  local copies, waits for them, and re-layouts  15.2 us (2%)
  between operations  10.6 us (1%)
    psum x3, blocking collectives, body(): gamma_new = jnp.sqrt(lax.psum(jnp.sum(zvec_new * vec_new), ('tm', 'space')))  194 us
    psum x3, blocking collectives, body(): delta = lax.psum(jnp.sum(image * zvec), ('tm', 'space'))  193 us
    psum x1, blocking collectives, body(): gamma = jnp.sqrt(lax.psum(jnp.sum(zvec * vec), ('tm', 'space')))  65 us
    all_to_all x3, blocking collectives, mirror(): lax.all_to_all(pieces, 'tm', split_axis=1, concat_axis=1, tiled=True)  55.7 us
    ppermute x16, starting transfers between devices, padded_2(): before = lax.ppermute(last, axis, up)  45.5 us
    ppermute x16, waiting for transfers between devices, padded_2(): after = lax.ppermute(leading, axis, down)  43.7 us
    all_to_all x3, blocking collectives, turn_back(): lax.all_to_all(reversed_pieces, 'tm', split_axis=1, concat_axis=1, tiled=...  40.9 us
    ppermute x16, starting transfers between devices, padded_2(): after = lax.ppermute(leading, axis, down)  36.1 us
  transfers between devices with their start and end apart: 37, of which 19 were waited for; matrix products, arithmetic and copies ran while one was open for 1% of the time, Pallas kernels for 0%

commit v1 on v0

v1 whole, which is shorter than its diff:
```python
import jax
import jax.numpy as jnp
from jax import lax
from jax.experimental import pallas as pl
from jax.experimental.pallas import tpu as pltpu
from jax.sharding import PartitionSpec as P

STEPS = 8
STRIPS = 16
BLOCKS = STEPS * STRIPS
LANES = 128
HALO = 16
WIDE = LANES + 2 * HALO
PAD = 8
TALL = WIDE + 2 * PAD
TILES = WIDE // 8
SEND = 12
BACK = 25


def lane_of(shape):
    return lax.broadcasted_iota(jnp.int32, shape, 1)


def row_of(shape):
    return lax.broadcasted_iota(jnp.int32, shape, 0)


def pack_kernel(step_ref, f_ref, k_ref, out_ref):
    step = step_ref[0]
    shift = lax.rem(jnp.int32(48) - 32 * step + 256, jnp.int32(128))
    lane = lane_of((8, LANES))
    zero = jnp.zeros((8, LANES), jnp.float32)

    def tile(ref, d):
        return ref[:, d * LANES : (d + 1) * LANES]

    def rolled(d):
        if d < 0 or d >= BLOCKS:
            return zero, zero
        return pltpu.roll(tile(f_ref, d), 16, 1), pltpu.roll(tile(k_ref, d), shift, 1)

    first, last = step == 0, step == 4
    before, here = rolled(-1), rolled(0)
    for d in range(BLOCKS):
        after = rolled(d + 1)
        lower = jnp.where(first, before[1], here[1])
        upper = jnp.where(last, after[1], here[1])
        side = jnp.where(lane < 16, before[0], jnp.where(lane < 32, after[0], jnp.where(lane < 48, lower, upper)))
        folded = jnp.where(lane < 64, side, pltpu.roll(pltpu.roll(side, 64, 1), 4, 0))
        out_ref[d * SEND : d * SEND + 8, :] = tile(f_ref, d)
        out_ref[d * SEND + 8 : d * SEND + 12, :] = folded[:4]
        before, here = here, after


def main_kernel(block_ref, in_ref, out_ref, sides, k, s, gn, gw, r0, r1, a, b, q0, q1, q2):
    lane = lane_of((8, LANES))
    sub = row_of((8, LANES))
    edge = jnp.zeros((PAD, LANES), jnp.float32)
    for ref in (k, s, gn, gw):
        ref[0:PAD, :] = edge
        ref[PAD + WIDE : TALL, :] = edge
    for ref in (r0, r1, a, b, q0, q1, q2):
        for t in range(STEPS):
            ref[t, 0:PAD, :] = edge
            ref[t, PAD + WIDE : TALL, :] = edge

    for t in range(STEPS):
        rows = []
        for i in range(STRIPS):
            at = SEND * (STRIPS * t + i)
            rows.append(in_ref[at : at + 8, :])
            piece = in_ref[at + 8 : at + 12, :]
            sides[8 * i : 8 * i + 4, :] = piece
            sides[8 * i + 4 : 8 * i + 8, :] = pltpu.roll(piece, 64, 1)
        r0[t, PAD + HALO : PAD + HALO + LANES, :] = jnp.concatenate(rows, 0).T
        turned = sides[...].T
        r0[t, PAD : PAD + HALO, :] = turned[0:16]
        r0[t, PAD + HALO + LANES : PAD + WIDE, :] = turned[16:32]
        if t < 5:
            k[PAD + 32 * t : PAD + 32 * t + 32, :] = turned[32:64]

    def at(i, offset=0):
        return pl.ds(pl.multiple_of(8 * i + PAD, 8) + offset, 8)

    def halves(i):
        mid = k[at(i), :]
        up = jnp.where(lane == 0, 0.0, pltpu.roll(mid, 1, 1))
        return mid, 0.5 * (mid + up), 0.5 * (mid + k[at(i, -1), :])

    @pl.loop(0, TILES)
    def _(i):
        mid, north, west = halves(i)
        down = jnp.where(lane == LANES - 1, 0.0, pltpu.roll(mid, LANES - 1, 1))
        south = 0.5 * (mid + down)
        east = 0.5 * (mid + k[at(i, 1), :])
        scale = 1.0 / jnp.sqrt(1.0 + north + south + west + east)
        s[at(i), :] = scale
        for t in range(STEPS):
            r0[t, at(i), :] = scale * r0[t, at(i), :]

    origin = block_ref[0] * LANES - HALO

    @pl.loop(0, TILES)
    def _(i):
        _, north, west = halves(i)
        scale = s[at(i), :]
        column = origin + 8 * i + sub
        inside = (column > 0) & (column < BLOCKS * LANES)
        gn[at(i), :] = jnp.where(lane == 0, 0.0, north * scale * pltpu.roll(scale, 1, 1))
        gw[at(i), :] = jnp.where(inside, west * scale * s[at(i, -1), :], 0.0)

    def sweep(src, low, high, emit, count):
        def one(i, sums):
            north, west, east = gn[at(i), :], gw[at(i), :], gw[at(i, 1), :]
            xs, gs = [], []
            for t in range(STEPS):
                x = src[t, at(i), :]
                left, right = src[t, at(i, -1), :], src[t, at(i, 1), :]
                total = north * pltpu.roll(x, 1, 1) + pltpu.roll(north * x, LANES - 1, 1)
                xs.append(x)
                gs.append(total + (west * left + east * right))
            terms = emit(i, xs, gs)
            own = (i >= HALO // 8) & (i < (HALO + LANES) // 8)
            return tuple(c + jnp.where(own, v, 0.0) for c, v in zip(sums, terms))

        zero = jnp.zeros((8, LANES), jnp.float32)
        return lax.fori_loop(low, high, one, (zero,) * count)

    def added(values):
        while len(values) > 1:
            values = [v + w for v, w in zip(values[::2], values[1::2])]
        return values[0]

    def product(left, right):
        return added([v * w for v, w in zip(left, right)])

    def every(ref, i):
        return [ref[t, at(i), :] for t in range(STEPS)]

    def put(ref, i, values):
        for t in range(STEPS):
            ref[t, at(i), :] = values[t]

    def polynomial(src, dst, bounds, emit, count):
        def start(i, xs, gs):
            put(a, i, [0.5 * (g + x) for x, g in zip(xs, gs)])
            return ()

        def middle(i, xs, gs):
            put(b, i, [g + 0.125 * v for v, g in zip(every(src, i), gs)])
            return ()

        def end(i, xs, gs):
            given = every(src, i)
            made = [g + 0.75 * v for v, g in zip(given, gs)]
            put(dst, i, made)
            return emit(i, given, made)

        sweep(src, *bounds[0], start, 0)
        sweep(a, *bounds[1], middle, 0)
        return sweep(b, *bounds[2], end, count)

    def operate(src, dst, bounds, later, emit, count):
        def act(i, xs, gs):
            inverse = s[at(i), :] * s[at(i), :]
            made = []
            for t in range(STEPS):
                other = t + 1 if later else t - 1
                value = xs[t] - gs[t]
                made.append(value - inverse * xs[other] if 0 <= other < STEPS else value)
            put(dst, i, made)
            return emit(xs, made)

        return sweep(src, *bounds, act, count)

    full, most = (0, TILES), (1, TILES - 1)
    (m0,) = polynomial(r0, q0, (full, full, full), lambda i, v, q: (product(v, q),), 1)
    (m1,) = operate(q0, r1, full, True, lambda x, r: (product(r, x[::-1]),), 1)
    (m2,) = polynomial(r1, q1, (full, most, most), lambda i, v, q: (product(v, q),), 1)
    operate(q1, r0, most, False, lambda x, r: (), 0)
    m4, m3 = polynomial(r0, q2, (most, most, most), lambda i, v, q: (product(v, q), product(every(r1, i), q[::-1])), 2)
    (m5,) = operate(q2, a, most, True, lambda x, r: (product(r, x[::-1]),), 1)

    def square(i, xs, gs):
        put(b, i, gs)
        return (added([x * (0.75 * x + 0.125 * g) + 0.5 * (g * g) for x, g in zip(xs, gs)]),)

    (m6,) = sweep(a, *most, square, 1)
    (m7,) = sweep(b, 2, TILES - 2, lambda i, xs, gs: (0.5 * product(xs, gs),), 1)

    moments = jnp.zeros((8, LANES), jnp.float32)
    for n, value in enumerate((m0, m1, m2, m3, m4, m5, m6 + m7)):
        moments = jnp.where(sub == n, jnp.sum(value, axis=0, keepdims=True), moments)
    totals = jnp.sum(moments, axis=1, keepdims=True)
    line = jnp.sum(jnp.where(lane == sub, totals, 0.0), axis=0, keepdims=True)

    own = slice(PAD + HALO, PAD + HALO + LANES)
    for t in range(STEPS):
        for field, (ref, step) in enumerate(((q0, STEPS - 1 - t), (q1, t), (q2, STEPS - 1 - t))):
            turned = (s[own, :] * ref[step, own, :]).T
            for i in range(STRIPS):
                to = BACK * (STRIPS * t + i) + 8 * field
                out_ref[to : to + 8, :] = turned[8 * i : 8 * i + 8]
    for d in range(BLOCKS):
        out_ref[BACK * d + 24 : BACK * d + 25, :] = line


def coefficients(m):
    def combined(p, q, shift):
        total = None
        for i, x in enumerate(p):
            for j, y in enumerate(q):
                if x is not None and y is not None:
                    term = x * y * m[i + j + shift]
                    total = term if total is None else total + term
        return total

    def plus(*pairs):
        made = []
        for entries in zip(*[v for _, v in pairs]):
            total = None
            for (factor, _), e in zip(pairs, entries):
                if e is not None and factor is not None:
                    total = factor * e if total is None else total + factor * e
            made.append(total)
        return made

    one = jnp.ones_like(m[0])
    nil = jnp.zeros_like(m[0])
    none = [None] * 4
    vec, vec_old = [one, None, None, None], none
    gamma, gamma_old = jnp.sqrt(m[0]), one
    w, w_old, x = none, none, none
    c = c_old = one
    s = s_old = nil
    eta = gamma
    for _ in range(3):
        z = plus((1.0 / gamma, vec))
        image = [None] + z[:3]
        delta = combined(z, z, 1)
        new = plus((one, image), (-delta / gamma, vec), (-gamma / gamma_old, vec_old))
        gamma_new = jnp.sqrt(jnp.maximum(combined(new, new, 0), 0.0))
        a0 = c * delta - c_old * s * gamma
        a1 = jnp.sqrt(a0 * a0 + gamma_new * gamma_new)
        a2 = s * delta + c_old * c * gamma
        a3 = s_old * gamma
        c_new, s_new = a0 / a1, gamma_new / a1
        w_new = plus((1.0 / a1, z), (-a3 / a1, w_old), (-a2 / a1, w))
        x = plus((one, x), (c_new * eta, w_new))
        eta = -s_new * eta
        vec_old, vec, gamma_old, gamma = vec, new, gamma, gamma_new
        w_old, w, c_old, c, s_old, s = w, w_new, c, c_new, s, s_new
    return x[:3]


def final_kernel(in_ref, out_ref):
    total = jnp.zeros((8, LANES), jnp.float32)
    for j in range(BLOCKS // 8):
        total = total + in_ref[pl.ds(24 + 8 * BACK * j, 8, stride=BACK), :]
    lane = lane_of((8, LANES))
    line = jnp.broadcast_to(jnp.sum(total, axis=0, keepdims=True), (8, LANES))
    m = [jnp.broadcast_to(jnp.sum(jnp.where(lane == n, line, 0.0), axis=1, keepdims=True), (8, LANES)) for n in range(7)]
    x0, x1, x2 = coefficients(m)
    for d in range(BLOCKS):
        at = BACK * d
        first, second, third = in_ref[at : at + 8, :], in_ref[at + 8 : at + 16, :], in_ref[at + 16 : at + 24, :]
        out_ref[:, d * LANES : (d + 1) * LANES] = x0 * first + x1 * second + x2 * third


def exchanged(blocks, rows):
    pieces = blocks.reshape(-1).reshape(BLOCKS, rows, 1, LANES)
    moved = lax.all_to_all(pieces, ("tm", "space"), split_axis=0, concat_axis=0)
    return moved.reshape(-1).reshape(BLOCKS * rows, LANES)


def body(forcing, conductivity):
    columns = forcing.shape[2]
    step = lax.axis_index("tm").astype(jnp.int32)
    block = step * STRIPS + lax.axis_index("space").astype(jnp.int32)
    scalar, whole = pl.BlockSpec(memory_space=pltpu.SMEM), pl.BlockSpec(memory_space=pltpu.VMEM)
    params = pltpu.CompilerParams(vmem_limit_bytes=40 * 2**20)
    packed = pl.pallas_call(
        pack_kernel,
        out_shape=jax.ShapeDtypeStruct((BLOCKS * SEND, LANES), jnp.float32),
        in_specs=[scalar, whole, whole],
        out_specs=whole,
        compiler_params=params,
        name="pack",
    )(step.reshape(1), forcing.reshape(8, columns), conductivity)
    flat, field = pltpu.VMEM((TALL, LANES), jnp.float32), pltpu.VMEM((STEPS, TALL, LANES), jnp.float32)
    basis = pl.pallas_call(
        main_kernel,
        out_shape=jax.ShapeDtypeStruct((BLOCKS * BACK, LANES), jnp.float32),
        in_specs=[scalar, whole],
        out_specs=whole,
        scratch_shapes=[pltpu.VMEM((LANES, LANES), jnp.float32)] + [flat] * 4 + [field] * 7,
        compiler_params=params,
        name="basis",
    )(block.reshape(1), exchanged(packed, SEND))
    out = pl.pallas_call(
        final_kernel,
        out_shape=jax.ShapeDtypeStruct((8, columns), jnp.float32),
        in_specs=[whole],
        out_specs=whole,
        compiler_params=params,
        name="combine",
    )(exchanged(basis, BACK))
    return out.reshape(1, 8, columns)


def solution(mesh):
    return jax.shard_map(
        body,
        mesh=mesh,
        in_specs=(P("tm", "space", None), P("space", None)),
        out_specs=P("tm", "space", None),
        check_vma=False,
    )
```

time: 863 us -> 96.4 us (0.11); the launches traced: 853 us -> 96.1 us
  blocking collectives: 548 us -> 29.9 us
  other arithmetic: 103 us -> 0 us
  starting transfers between devices: 97 us -> 11.5 us
  waiting for transfers between devices: 79.2 us -> 16.2 us
  Pallas kernels: 0 us -> 36.4 us
  local copies, waits for them, and re-layouts: 15.2 us -> 2.08 us
  between operations: 10.6 us -> 0.02 us
    psum x7 -> x0, blocking collectives: 451 us -> none  [the longest x3 194 us: body(): gamma_new = jnp.sqrt(lax.psum(jnp.sum(zvec_new * vec_new), ('tm', 'space')))]
    ppermute x35 -> x0, starting transfers between devices: 87.2 us -> none  [the longest x16 45.5 us: padded_2(): before = lax.ppermute(last, axis, up)]
    all_to_all x6 -> x1, blocking collectives: 96.6 us -> 29.9 us  [exchanged(): moved = lax.all_to_all(pieces, ('tm', 'space'), split_axis=0, concat_axis=0)]
    ppermute x35 -> x0, waiting for transfers between devices: 63.2 us -> none  [the longest x16 43.7 us: padded_2(): after = lax.ppermute(leading, axis, down)]
    pallas_call x0 -> x3, Pallas kernels: none -> 36.4 us  [the longest x1 28.3 us: body(): pl.pallas_call(main_kernel, out_shape=jax.ShapeDtypeStruct((BLOCKS * BACK...]
    concatenate x16 -> x0, other arithmetic: 31.1 us -> none  [padded_2(): x = jnp.concatenate([before, x, after], axis=dim)]
    reduce_sum x7 -> x0, other arithmetic: 27.4 us -> none  [the longest x3 17.5 us: body(): gamma_new = jnp.sqrt(lax.psum(jnp.sum(zvec_new * vec_new), ('tm', 'space')))]
    mul x13 -> x0, other arithmetic: 25.9 us -> none  [the longest x10 21.5 us: apply_step(): inner = padded_2(scale * term, (('space', 1),), 1)]
  transfers between devices with their start and end apart: 37 -> 1, of which waited for: 19 -> 1; matrix products, arithmetic and copies ran while one was open for 1% -> 0% of each run, Pallas kernels for 0% -> 0%
where the time goes in v1:
time: 96.4 us; the launch traced here: 96.1 us
  Pallas kernels  36.4 us (38%)
  blocking collectives  29.9 us (31%)
  waiting for transfers between devices  16.2 us (17%)
  starting transfers between devices  11.5 us (12%)
  local copies, waits for them, and re-layouts  2.08 us (2%)
    all_to_all x1, blocking collectives, exchanged(): moved = lax.all_to_all(pieces, ('tm', 'space'), split_axis=0, concat_axis=0)  29.9 us
    pallas_call x1, Pallas kernels, body(): pl.pallas_call(main_kernel, out_shape=jax.ShapeDtypeStruct((BLOCKS * BACK...  28.3 us
    all_to_all x1, waiting for transfers between devices, exchanged(): moved = lax.all_to_all(pieces, ('tm', 'space'), split_axis=0, concat_axis=0)  16.2 us
    all_to_all x1, starting transfers between devices, exchanged(): moved = lax.all_to_all(pieces, ('tm', 'space'), split_axis=0, concat_axis=0)  11.5 us
    pallas_call x1, Pallas kernels, body(): pl.pallas_call(pack_kernel, out_shape=jax.ShapeDtypeStruct((BLOCKS * SEND...  6.99 us
    unnamed x4, local copies, waits for them, and re-layouts  2.08 us
  transfers between devices with their start and end apart: 1, of which 1 were waited for; matrix products, arithmetic and copies ran while one was open for 0% of the time, Pallas kernels for 0%

profile of v1, /device:TPU:1, one launch (start us, length us, event | category | flops | bytes accessed | tf_op | source)
XLA Modules:
  0.0 96.1 jit_solution(585417019004924967)
XLA Ops:
  0.0 0.0 copy-start
  0.0 1.0 %copy-done = f32[1,8,16384]{2,1,0:T(8,128)S(1)} copy-done((f32[1,8,16384]{2,1,0:T(8,128)S(1)}, f32[1,8,16384]{2,1,0:T(8,128)}, u32[]{:S(2)}) %copy-start) | copy-done | bytes 524312
  1.0 0.0 copy-start.1
  1.0 1.0 %copy-done.1 = f32[8,16384]{1,0:T(8,128)S(1)} copy-done((f32[8,16384]{1,0:T(8,128)S(1)}, f32[8,16384]{1,0:T(8,128)}, u32[]{:S(2)}) %copy-start.1) | copy-done | bytes 524312
  2.1 7.0 %pack.1 = f32[1536,128]{1,0:T(8,128)} custom-call(s32[1]{0:T(128)} %bitcast.1.step_ref, f32[8,16384]{1,0:T(8,128)S(1)} %bitcast.11, f32[8,16384]{1,0:T(8,128)S(1)} %copy-done.1), custom_call_target="tpu_custom_call" | custom-call | tf_op jit(solution)/shard_map/pack/pallas_call | solution.py:283
  9.1 11.5 %all-to-all-start = ((f32[128,12,1,128]{3,2,1,0:T(1,128)}), f32[128,12,1,128]{3,2,1,0:T(1,128)S(1)}, u32[]{:S(2)}, u32[]{:S(2)}) async-start(f32[128,12,1,128]{3,2,1,0:T(1,128)} %bitcast.3), calls=%async_computation | async-start | bytes 1572864 | tf_op jit(solution)/shard_map/all_to_all | solution.py:273
  20.6 16.2 %all-to-all-done = f32[128,12,1,128]{3,2,1,0:T(1,128)S(1)} async-done(((f32[128,12,1,128]{3,2,1,0:T(1,128)}), f32[128,12,1,128]{3,2,1,0:T(1,128)S(1)}, u32[]{:S(2)}, u32[]{:S(2)}) %all-to-all-start) | async-done | bytes 786464 | tf_op jit(solution)/shard_map/all_to_all | solution.py:273
  36.8 28.3 %basis.1 = f32[3200,128]{1,0:T(8,128)S(1)} custom-call(s32[1]{0:T(128)} %bitcast.block_ref, f32[1536,128]{1,0:T(8,128)S(1)} %bitcast.10), custom_call_target="tpu_custom_call" | custom-call | tf_op jit(solution)/shard_map/basis/pallas_call | solution.py:292
  65.1 29.9 %all_to_all.10 = f32[128,25,1,128]{3,2,1,0:T(1,128)S(1)} all-to-all(f32[128,25,1,128]{3,2,1,0:T(1,128)S(1)} %bitcast.8), channel_id=1, replica_groups=mesh['tm'=8,'space'=16] {'tm','space'}, dimensions={0} | all-to-all | bytes 3276800 | tf_op jit(solution)/shard_map/all_to_all | solution.py:273
  95.0 1.1 %combine.1 = f32[8,16384]{1,0:T(8,128)} custom-call(f32[3200,128]{1,0:T(8,128)S(1)} %bitcast.9), custom_call_target="tpu_custom_call" | custom-call | tf_op jit(solution)/shard_map/combine/pallas_call | solution.py:301
Async XLA Ops:
  0.0 1.0 %copy-start = (f32[1,8,16384]{2,1,0:T(8,128)S(1)}, f32[1,8,16384]{2,1,0:T(8,128)}, u32[]{:S(2)}) copy-start(f32[1,8,16384]{2,1,0:T(8,128)} %param.2) | copy-start | bytes 1572868
  1.0 1.0 %copy-start.1 = (f32[8,16384]{1,0:T(8,128)S(1)}, f32[8,16384]{1,0:T(8,128)}, u32[]{:S(2)}) copy-start(f32[8,16384]{1,0:T(8,128)} %k_ref.1) | copy-start | bytes 1572868
  9.1 27.7 %all-to-all-start = ((f32[128,12,1,128]{3,2,1,0:T(1,128)}), f32[128,12,1,128]{3,2,1,0:T(1,128)S(1)}, u32[]{:S(2)}, u32[]{:S(2)}) async-start(f32[128,12,1,128]{3,2,1,0:T(1,128)} %bitcast.3), calls=%async_computation | async-start | bytes 1572864 | tf_op jit(solution)/shard_map/all_to_all | solution.py:273

commit v2 on v1

--- a/solution.py
+++ b/solution.py
@@ -26,9 +26,10 @@
     return lax.broadcasted_iota(jnp.int32, shape, 0)
 
 
-def pack_kernel(step_ref, f_ref, k_ref, out_ref):
+def pack_kernel(step_ref, f_ref, k_ref, out_ref, side_ref):
     step = step_ref[0]
     shift = lax.rem(jnp.int32(48) - 32 * step + 256, jnp.int32(128))
+    first, last = step == 0, step == 4
     lane = lane_of((8, LANES))
     zero = jnp.zeros((8, LANES), jnp.float32)
 
@@ -40,30 +41,33 @@
             return zero, zero
         return pltpu.roll(tile(f_ref, d), 16, 1), pltpu.roll(tile(k_ref, d), shift, 1)
 
-    first, last = step == 0, step == 4
     before, here = rolled(-1), rolled(0)
     for d in range(BLOCKS):
         after = rolled(d + 1)
         lower = jnp.where(first, before[1], here[1])
         upper = jnp.where(last, after[1], here[1])
-        side = jnp.where(lane < 16, before[0], jnp.where(lane < 32, after[0], jnp.where(lane < 48, lower, upper)))
-        folded = jnp.where(lane < 64, side, pltpu.roll(pltpu.roll(side, 64, 1), 4, 0))
+        side_ref[8 * d : 8 * d + 8, :] = jnp.where(
+            lane < 16, before[0], jnp.where(lane < 32, after[0], jnp.where(lane < 48, lower, upper))
+        )
         out_ref[d * SEND : d * SEND + 8, :] = tile(f_ref, d)
-        out_ref[d * SEND + 8 : d * SEND + 12, :] = folded[:4]
         before, here = here, after
+    for d in range(BLOCKS):
+        upper, lower = side_ref[8 * d : 8 * d + 4, :], side_ref[8 * d + 4 : 8 * d + 8, :]
+        folded = jnp.where(lane[:4] < 64, upper, pltpu.roll(lower, 64, 1))
+        out_ref[d * SEND + 8 : d * SEND + 12, :] = folded
 
 
 def main_kernel(block_ref, in_ref, out_ref, sides, k, s, gn, gw, r0, r1, a, b, q0, q1, q2):
     lane = lane_of((8, LANES))
     sub = row_of((8, LANES))
     edge = jnp.zeros((PAD, LANES), jnp.float32)
+    edges = jnp.zeros((STEPS, PAD, LANES), jnp.float32)
     for ref in (k, s, gn, gw):
         ref[0:PAD, :] = edge
         ref[PAD + WIDE : TALL, :] = edge
     for ref in (r0, r1, a, b, q0, q1, q2):
-        for t in range(STEPS):
-            ref[t, 0:PAD, :] = edge
-            ref[t, PAD + WIDE : TALL, :] = edge
+        ref[:, 0:PAD, :] = edges
+        ref[:, PAD + WIDE : TALL, :] = edges
 
     for t in range(STEPS):
         rows = []
@@ -88,7 +92,7 @@
         up = jnp.where(lane == 0, 0.0, pltpu.roll(mid, 1, 1))
         return mid, 0.5 * (mid + up), 0.5 * (mid + k[at(i, -1), :])
 
-    @pl.loop(0, TILES)
+    @pl.loop(0, TILES, unroll=True)
     def _(i):
         mid, north, west = halves(i)
         down = jnp.where(lane == LANES - 1, 0.0, pltpu.roll(mid, LANES - 1, 1))
@@ -96,12 +100,11 @@
         east = 0.5 * (mid + k[at(i, 1), :])
         scale = 1.0 / jnp.sqrt(1.0 + north + south + west + east)
         s[at(i), :] = scale
-        for t in range(STEPS):
-            r0[t, at(i), :] = scale * r0[t, at(i), :]
+        r0[:, at(i), :] = scale * r0[:, at(i), :]
 
     origin = block_ref[0] * LANES - HALO
 
-    @pl.loop(0, TILES)
+    @pl.loop(0, TILES, unroll=True)
     def _(i):
         _, north, west = halves(i)
         scale = s[at(i), :]
@@ -113,48 +116,31 @@
     def sweep(src, low, high, emit, count):
         def one(i, sums):
             north, west, east = gn[at(i), :], gw[at(i), :], gw[at(i, 1), :]
-            xs, gs = [], []
-            for t in range(STEPS):
-                x = src[t, at(i), :]
-                left, right = src[t, at(i, -1), :], src[t, at(i, 1), :]
-                total = north * pltpu.roll(x, 1, 1) + pltpu.roll(north * x, LANES - 1, 1)
-                xs.append(x)
-                gs.append(total + (west * left + east * right))
-            terms = emit(i, xs, gs)
+            x, left, right = src[:, at(i), :], src[:, at(i, -1), :], src[:, at(i, 1), :]
+            g = north * pltpu.roll(x, 1, 2) + pltpu.roll(north * x, LANES - 1, 2)
+            terms = emit(i, x, g + (west * left + east * right))
             own = (i >= HALO // 8) & (i < (HALO + LANES) // 8)
-            return tuple(c + jnp.where(own, v, 0.0) for c, v in zip(sums, terms))
+            return tuple(c + jnp.where(own, jnp.sum(v, axis=0), 0.0) for c, v in zip(sums, terms))
 
         zero = jnp.zeros((8, LANES), jnp.float32)
-        return lax.fori_loop(low, high, one, (zero,) * count)
-
-    def added(values):
-        while len(values) > 1:
-            values = [v + w for v, w in zip(values[::2], values[1::2])]
-        return values[0]
-
-    def product(left, right):
-        return added([v * w for v, w in zip(left, right)])
-
-    def every(ref, i):
-        return [ref[t, at(i), :] for t in range(STEPS)]
-
-    def put(ref, i, values):
-        for t in range(STEPS):
-            ref[t, at(i), :] = values[t]
+        return lax.fori_loop(low, high, one, (zero,) * count, unroll=True)
+
+    def turned_in_time(x):
+        return jnp.concatenate([x[t : t + 1] for t in reversed(range(STEPS))], 0)
 
     def polynomial(src, dst, bounds, emit, count):
-        def start(i, xs, gs):
-            put(a, i, [0.5 * (g + x) for x, g in zip(xs, gs)])
+        def start(i, x, g):
+            a[:, at(i), :] = 0.5 * (g + x)
             return ()
 
-        def middle(i, xs, gs):
-            put(b, i, [g + 0.125 * v for v, g in zip(every(src, i), gs)])
+        def middle(i, x, g):
+            b[:, at(i), :] = g + 0.125 * src[:, at(i), :]
             return ()
 
-        def end(i, xs, gs):
-            given = every(src, i)
-            made = [g + 0.75 * v for v, g in zip(given, gs)]
-            put(dst, i, made)
+        def end(i, x, g):
+            given = src[:, at(i), :]
+            made = g + 0.75 * given
+            dst[:, at(i), :] = made
             return emit(i, given, made)
 
         sweep(src, *bounds[0], start, 0)
@@ -162,32 +148,39 @@
         return sweep(b, *bounds[2], end, count)
 
     def operate(src, dst, bounds, later, emit, count):
-        def act(i, xs, gs):
+        nothing = jnp.zeros((1, 8, LANES), jnp.float32)
+
+        def act(i, x, g):
             inverse = s[at(i), :] * s[at(i), :]
-            made = []
-            for t in range(STEPS):
-                other = t + 1 if later else t - 1
-                value = xs[t] - gs[t]
-                made.append(value - inverse * xs[other] if 0 <= other < STEPS else value)
-            put(dst, i, made)
-            return emit(xs, made)
+            other = jnp.concatenate([x[1:], nothing] if later else [nothing, x[:-1]], 0)
+            made = x - g - inverse * other
+            dst[:, at(i), :] = made
+            return emit(x, made)
 
         return sweep(src, *bounds, act, count)
 
+    def same(i, v, q):
+        return (v * q,)
+
+    def mirrored(x, r):
+        return (r * turned_in_time(x),)
+
     full, most = (0, TILES), (1, TILES - 1)
-    (m0,) = polynomial(r0, q0, (full, full, full), lambda i, v, q: (product(v, q),), 1)
-    (m1,) = operate(q0, r1, full, True, lambda x, r: (product(r, x[::-1]),), 1)
-    (m2,) = polynomial(r1, q1, (full, most, most), lambda i, v, q: (product(v, q),), 1)
+    (m0,) = polynomial(r0, q0, (full, full, full), same, 1)
+    (m1,) = operate(q0, r1, full, True, mirrored, 1)
+    (m2,) = polynomial(r1, q1, (full, most, most), same, 1)
     operate(q1, r0, most, False, lambda x, r: (), 0)
-    m4, m3 = polynomial(r0, q2, (most, most, most), lambda i, v, q: (product(v, q), product(every(r1, i), q[::-1])), 2)
-    (m5,) = operate(q2, a, most, True, lambda x, r: (product(r, x[::-1]),), 1)
-
-    def square(i, xs, gs):
-        put(b, i, gs)
-        return (added([x * (0.75 * x + 0.125 * g) + 0.5 * (g * g) for x, g in zip(xs, gs)]),)
+    m4, m3 = polynomial(
+        r0, q2, (most, most, most), lambda i, v, q: (v * q, r1[:, at(i), :] * turned_in_time(q)), 2
+    )
+    (m5,) = operate(q2, a, most, True, mirrored, 1)
+
+    def square(i, x, g):
+        b[:, at(i), :] = g
+        return (x * (0.75 * x + 0.125 * g) + 0.5 * (g * g),)
 
     (m6,) = sweep(a, *most, square, 1)
-    (m7,) = sweep(b, 2, TILES - 2, lambda i, xs, gs: (0.5 * product(xs, gs),), 1)
+    (m7,) = sweep(b, 2, TILES - 2, lambda i, x, g: (0.5 * (x * g),), 1)
 
     moments = jnp.zeros((8, LANES), jnp.float32)
     for n, value in enumerate((m0, m1, m2, m3, m4, m5, m6 + m7)):
@@ -285,6 +278,7 @@
         out_shape=jax.ShapeDtypeStruct((BLOCKS * SEND, LANES), jnp.float32),
         in_specs=[scalar, whole, whole],
         out_specs=whole,
+        scratch_shapes=[pltpu.VMEM((BLOCKS * 8, LANES), jnp.float32)],
         compiler_params=params,
         name="pack",
     )(step.reshape(1), forcing.reshape(8, columns), conductivity)

time: 96.4 us -> 68.2 us (0.71)
  Pallas kernels: 36.4 us -> 8.22 us
    pallas_call x1, Pallas kernels: 28.3 us -> 5.74 us  [body(): pl.pallas_call(main_kernel, out_shape=jax.ShapeDtypeStruct((BLOCKS * BACK...]
    pallas_call x1, Pallas kernels: 6.99 us -> 1.36 us  [body(): pl.pallas_call(pack_kernel, out_shape=jax.ShapeDtypeStruct((BLOCKS * SEND...]
where the time goes in v2:
time: 68.2 us; the launch traced here: 67.9 us
  blocking collectives  29.9 us (44%)
  waiting for transfers between devices  16.2 us (24%)
  starting transfers between devices  11.5 us (17%)
  Pallas kernels  8.22 us (12%)
  local copies, waits for them, and re-layouts  2.08 us (3%)
    all_to_all x1, blocking collectives, exchanged(): moved = lax.all_to_all(pieces, ('tm', 'space'), split_axis=0, concat_axis=0)  29.9 us
    all_to_all x1, waiting for transfers between devices, exchanged(): moved = lax.all_to_all(pieces, ('tm', 'space'), split_axis=0, concat_axis=0)  16.2 us
    all_to_all x1, starting transfers between devices, exchanged(): moved = lax.all_to_all(pieces, ('tm', 'space'), split_axis=0, concat_axis=0)  11.5 us
    pallas_call x1, Pallas kernels, body(): pl.pallas_call(main_kernel, out_shape=jax.ShapeDtypeStruct((BLOCKS * BACK...  5.74 us
    unnamed x4, local copies, waits for them, and re-layouts  2.08 us
  transfers between devices with their start and end apart: 1, of which 1 were waited for; matrix products, arithmetic and copies ran while one was open for 0% of the time, Pallas kernels for 0%

profile of v2, /device:TPU:1, one launch (start us, length us, event | category | flops | bytes accessed | tf_op | source)
XLA Modules:
  0.0 67.9 jit_solution(5495802183762690445)
XLA Ops:
  0.0 0.0 copy-start
  0.0 1.0 %copy-done = f32[1,8,16384]{2,1,0:T(8,128)S(1)} copy-done((f32[1,8,16384]{2,1,0:T(8,128)S(1)}, f32[1,8,16384]{2,1,0:T(8,128)}, u32[]{:S(2)}) %copy-start) | copy-done | bytes 524312
  1.0 0.0 copy-start.1
  1.0 1.0 %copy-done.1 = f32[8,16384]{1,0:T(8,128)S(1)} copy-done((f32[8,16384]{1,0:T(8,128)S(1)}, f32[8,16384]{1,0:T(8,128)}, u32[]{:S(2)}) %copy-start.1) | copy-done | bytes 524312
  2.1 1.4 %pack.1 = f32[1536,128]{1,0:T(8,128)} custom-call(s32[1]{0:T(128)} %bitcast.1.step_ref, f32[8,16384]{1,0:T(8,128)S(1)} %bitcast.11, f32[8,16384]{1,0:T(8,128)S(1)} %copy-done.1), custom_call_target="tpu_custom_call" | custom-call | tf_op jit(solution)/shard_map/pack/pallas_call | solution.py:276
  3.4 11.5 %all-to-all-start = ((f32[128,12,1,128]{3,2,1,0:T(1,128)}), f32[128,12,1,128]{3,2,1,0:T(1,128)S(1)}, u32[]{:S(2)}, u32[]{:S(2)}) async-start(f32[128,12,1,128]{3,2,1,0:T(1,128)} %bitcast.3), calls=%async_computation | async-start | bytes 1572864 | tf_op jit(solution)/shard_map/all_to_all | solution.py:266
  15.0 16.2 %all-to-all-done = f32[128,12,1,128]{3,2,1,0:T(1,128)S(1)} async-done(((f32[128,12,1,128]{3,2,1,0:T(1,128)}), f32[128,12,1,128]{3,2,1,0:T(1,128)S(1)}, u32[]{:S(2)}, u32[]{:S(2)}) %all-to-all-start) | async-done | bytes 786464 | tf_op jit(solution)/shard_map/all_to_all | solution.py:266
  31.2 5.7 %basis.1 = f32[3200,128]{1,0:T(8,128)S(1)} custom-call(s32[1]{0:T(128)} %bitcast.block_ref, f32[1536,128]{1,0:T(8,128)S(1)} %bitcast.10), custom_call_target="tpu_custom_call" | custom-call | tf_op jit(solution)/shard_map/basis/pallas_call | solution.py:286
  36.9 29.9 %all_to_all.10 = f32[128,25,1,128]{3,2,1,0:T(1,128)S(1)} all-to-all(f32[128,25,1,128]{3,2,1,0:T(1,128)S(1)} %bitcast.8), channel_id=1, replica_groups=mesh['tm'=8,'space'=16] {'tm','space'}, dimensions={0} | all-to-all | bytes 3276800 | tf_op jit(solution)/shard_map/all_to_all | solution.py:266
  66.8 1.1 %combine.1 = f32[8,16384]{1,0:T(8,128)} custom-call(f32[3200,128]{1,0:T(8,128)S(1)} %bitcast.9), custom_call_target="tpu_custom_call" | custom-call | tf_op jit(solution)/shard_map/combine/pallas_call | solution.py:295
Async XLA Ops:
  0.0 1.0 %copy-start = (f32[1,8,16384]{2,1,0:T(8,128)S(1)}, f32[1,8,16384]{2,1,0:T(8,128)}, u32[]{:S(2)}) copy-start(f32[1,8,16384]{2,1,0:T(8,128)} %param.2) | copy-start | bytes 1572868
  1.0 1.0 %copy-start.1 = (f32[8,16384]{1,0:T(8,128)S(1)}, f32[8,16384]{1,0:T(8,128)}, u32[]{:S(2)}) copy-start(f32[8,16384]{1,0:T(8,128)} %k_ref.1) | copy-start | bytes 1572868
  3.4 27.7 %all-to-all-start = ((f32[128,12,1,128]{3,2,1,0:T(1,128)}), f32[128,12,1,128]{3,2,1,0:T(1,128)S(1)}, u32[]{:S(2)}, u32[]{:S(2)}) async-start(f32[128,12,1,128]{3,2,1,0:T(1,128)} %bitcast.3), calls=%async_computation | async-start | bytes 1572864 | tf_op jit(solution)/shard_map/all_to_all | solution.py:266

commit v3 on v2

--- a/solution.py
+++ b/solution.py
@@ -16,6 +16,8 @@
 TILES = WIDE // 8
 SEND = 12
 BACK = 25
+CHUNKS = 2
+LIMIT = 60
 
 
 def lane_of(shape):
@@ -26,8 +28,22 @@
     return lax.broadcasted_iota(jnp.int32, shape, 0)
 
 
-def pack_kernel(step_ref, f_ref, k_ref, out_ref, side_ref):
-    step = step_ref[0]
+def pack_kernel(place_ref, f_hbm, k_hbm, out_ref, f_ref, k_ref, side_ref, sems):
+    width = BLOCKS * LANES // CHUNKS
+    copies = []
+    for n in range(CHUNKS):
+        part = pl.ds(n * width, width)
+        copies.append(
+            [
+                pltpu.make_async_copy(source.at[:, part], target.at[:, part], sems.at[j, n])
+                for j, (source, target) in enumerate(((f_hbm, f_ref), (k_hbm, k_ref)))
+            ]
+        )
+    for pair in copies:
+        for copy in pair:
+            copy.start()
+
+    step = place_ref[0]
     shift = lax.rem(jnp.int32(48) - 32 * step + 256, jnp.int32(128))
     first, last = step == 0, step == 4
     lane = lane_of((8, LANES))
@@ -41,23 +57,29 @@
             return zero, zero
         return pltpu.roll(tile(f_ref, d), 16, 1), pltpu.roll(tile(k_ref, d), shift, 1)
 
-    before, here = rolled(-1), rolled(0)
-    for d in range(BLOCKS):
-        after = rolled(d + 1)
-        lower = jnp.where(first, before[1], here[1])
-        upper = jnp.where(last, after[1], here[1])
-        side_ref[8 * d : 8 * d + 8, :] = jnp.where(
-            lane < 16, before[0], jnp.where(lane < 32, after[0], jnp.where(lane < 48, lower, upper))
-        )
-        out_ref[d * SEND : d * SEND + 8, :] = tile(f_ref, d)
-        before, here = here, after
+    before, here, done = rolled(-1), None, 0
+    for n in range(CHUNKS):
+        for copy in copies[n]:
+            copy.wait()
+        ready = BLOCKS if n == CHUNKS - 1 else (n + 1) * BLOCKS // CHUNKS - 1
+        here = rolled(0) if n == 0 else here
+        for d in range(done, ready):
+            after = rolled(d + 1)
+            lower = jnp.where(first, before[1], here[1])
+            upper = jnp.where(last, after[1], here[1])
+            side_ref[8 * d : 8 * d + 8, :] = jnp.where(
+                lane < 16, before[0], jnp.where(lane < 32, after[0], jnp.where(lane < 48, lower, upper))
+            )
+            out_ref[d * SEND : d * SEND + 8, :] = tile(f_ref, d)
+            before, here = here, after
+        done = ready
     for d in range(BLOCKS):
         upper, lower = side_ref[8 * d : 8 * d + 4, :], side_ref[8 * d + 4 : 8 * d + 8, :]
         folded = jnp.where(lane[:4] < 64, upper, pltpu.roll(lower, 64, 1))
         out_ref[d * SEND + 8 : d * SEND + 12, :] = folded
 
 
-def main_kernel(block_ref, in_ref, out_ref, sides, k, s, gn, gw, r0, r1, a, b, q0, q1, q2):
+def main_kernel(place_ref, in_ref, out_ref, sides, k, s, gn, gw, r0, r1, a, b, q0, q1, q2):
     lane = lane_of((8, LANES))
     sub = row_of((8, LANES))
     edge = jnp.zeros((PAD, LANES), jnp.float32)
@@ -102,7 +124,7 @@
         s[at(i), :] = scale
         r0[:, at(i), :] = scale * r0[:, at(i), :]
 
-    origin = block_ref[0] * LANES - HALO
+    origin = (place_ref[0] * STRIPS + place_ref[1]) * LANES - HALO
 
     @pl.loop(0, TILES, unroll=True)
     def _(i):
@@ -269,19 +291,24 @@
 
 def body(forcing, conductivity):
     columns = forcing.shape[2]
-    step = lax.axis_index("tm").astype(jnp.int32)
-    block = step * STRIPS + lax.axis_index("space").astype(jnp.int32)
+    place = jnp.stack([lax.axis_index("tm"), lax.axis_index("space")]).astype(jnp.int32)
     scalar, whole = pl.BlockSpec(memory_space=pltpu.SMEM), pl.BlockSpec(memory_space=pltpu.VMEM)
+    held = pl.BlockSpec(memory_space=pl.ANY)
     params = pltpu.CompilerParams(vmem_limit_bytes=40 * 2**20)
     packed = pl.pallas_call(
         pack_kernel,
         out_shape=jax.ShapeDtypeStruct((BLOCKS * SEND, LANES), jnp.float32),
-        in_specs=[scalar, whole, whole],
+        in_specs=[scalar, held, held],
         out_specs=whole,
-        scratch_shapes=[pltpu.VMEM((BLOCKS * 8, LANES), jnp.float32)],
-        compiler_params=params,
+        scratch_shapes=[
+            pltpu.VMEM((8, columns), jnp.float32),
+            pltpu.VMEM((8, columns), jnp.float32),
+            pltpu.VMEM((BLOCKS * 8, LANES), jnp.float32),
+            pltpu.SemaphoreType.DMA((2, CHUNKS)),
+        ],
+        compiler_params=pltpu.CompilerParams(vmem_limit_bytes=LIMIT * 2**20),
         name="pack",
-    )(step.reshape(1), forcing.reshape(8, columns), conductivity)
+    )(place, forcing.reshape(8, columns), conductivity)
     flat, field = pltpu.VMEM((TALL, LANES), jnp.float32), pltpu.VMEM((STEPS, TALL, LANES), jnp.float32)
     basis = pl.pallas_call(
         main_kernel,
@@ -291,7 +318,7 @@
         scratch_shapes=[pltpu.VMEM((LANES, LANES), jnp.float32)] + [flat] * 4 + [field] * 7,
         compiler_params=params,
         name="basis",
-    )(block.reshape(1), exchanged(packed, SEND))
+    )(place, exchanged(packed, SEND))
     out = pl.pallas_call(
         final_kernel,
         out_shape=jax.ShapeDtypeStruct((8, columns), jnp.float32),

time: 68.2 us -> 69.1 us (1.013)
  blocking collectives: 29.9 us -> 57.6 us
  waiting for transfers between devices: 16.2 us -> 0 us
  starting transfers between devices: 11.5 us -> 0 us
  Pallas kernels: 8.22 us -> 10.7 us
  local copies, waits for them, and re-layouts: 2.08 us -> 0.01 us
    all_to_all x1 -> x2, blocking collectives: 29.9 us -> 57.6 us  [exchanged(): moved = lax.all_to_all(pieces, ('tm', 'space'), split_axis=0, concat_axis=0)]
    all_to_all x1 -> x0, waiting for transfers between devices: 16.2 us -> none  [exchanged(): moved = lax.all_to_all(pieces, ('tm', 'space'), split_axis=0, concat_axis=0)]
    all_to_all x1 -> x0, starting transfers between devices: 11.5 us -> none  [exchanged(): moved = lax.all_to_all(pieces, ('tm', 'space'), split_axis=0, concat_axis=0)]
    unnamed x4 -> x2, local copies, waits for them, and re-layouts: 2.08 us -> 0.01 us
    pallas_call x1, Pallas kernels: 1.36 us -> 3.3 us  [body(): pl.pallas_call(pack_kernel, out_shape=jax.ShapeDtypeStruct((BLOCKS * SEND...]
  transfers between devices with their start and end apart: 1 -> 0, of which waited for: 1 -> 0; matrix products, arithmetic and copies ran while one was open for 0% -> 0% of each run, Pallas kernels for 0% -> 0%
where the time goes in v3:
time: 69.1 us; the launch traced here: 68.9 us
  blocking collectives  57.6 us (83%)
  Pallas kernels  10.7 us (15%)
    all_to_all x2, blocking collectives, exchanged(): moved = lax.all_to_all(pieces, ('tm', 'space'), split_axis=0, concat_axis=0)  57.6 us
    pallas_call x1, Pallas kernels, body(): pl.pallas_call(main_kernel, out_shape=jax.ShapeDtypeStruct((BLOCKS * BACK...  6.28 us
    pallas_call x1, Pallas kernels, body(): pl.pallas_call(pack_kernel, out_shape=jax.ShapeDtypeStruct((BLOCKS * SEND...  3.3 us

profile of v3, /device:TPU:1, one launch (start us, length us, event | category | flops | bytes accessed | tf_op | source)
XLA Modules:
  0.0 68.9 jit_solution(12524017585520593081)
XLA Ops:
  0.0 0.6 pad_add_fusion.place_ref
  0.6 0.0 copy-start
  0.6 3.3 %pack.1 = f32[1536,128]{1,0:T(8,128)} custom-call(s32[2]{0:T(128)} %pad_add_fusion.place_ref, f32[8,16384]{1,0:T(8,128)} %bitcast.12, f32[8,16384]{1,0:T(8,128)} %k_hbm.1), custom_call_target="tpu_custom_call" | custom-call | tf_op jit(solution)/shard_map/pack/pallas_call | solution.py:298
  3.9 27.8 %all_to_all.10 = f32[128,12,1,128]{3,2,1,0:T(1,128)S(1)} all-to-all(f32[128,12,1,128]{3,2,1,0:T(1,128)} %bitcast.11), channel_id=1, replica_groups=mesh['tm'=8,'space'=16] {'tm','space'}, dimensions={0} | all-to-all | bytes 1572864 | tf_op jit(solution)/shard_map/all_to_all | solution.py:288
  31.6 0.0 copy-done
  31.6 6.3 %basis.1 = f32[3200,128]{1,0:T(8,128)S(1)} custom-call(s32[2]{0:T(128)S(1)} %copy-done, f32[1536,128]{1,0:T(8,128)S(1)} %bitcast.10), custom_call_target="tpu_custom_call" | custom-call | tf_op jit(solution)/shard_map/basis/pallas_call | solution.py:313
  37.9 29.9 %all_to_all.11 = f32[128,25,1,128]{3,2,1,0:T(1,128)S(1)} all-to-all(f32[128,25,1,128]{3,2,1,0:T(1,128)S(1)} %bitcast.8), channel_id=1, replica_groups=mesh['tm'=8,'space'=16] {'tm','space'}, dimensions={0} | all-to-all | bytes 3276800 | tf_op jit(solution)/shard_map/all_to_all | solution.py:288
  67.8 1.1 %combine.1 = f32[8,16384]{1,0:T(8,128)} custom-call(f32[3200,128]{1,0:T(8,128)S(1)} %bitcast.9), custom_call_target="tpu_custom_call" | custom-call | tf_op jit(solution)/shard_map/combine/pallas_call | solution.py:322
Async XLA Ops:
  0.6 31.1 %copy-start = (s32[2]{0:T(128)S(1)}, s32[2]{0:T(128)}, u32[]{:S(2)}) copy-start(s32[2]{0:T(128)} %pad_add_fusion.place_ref) | copy-start | bytes 28

commit v4 on v3

--- a/solution.py
+++ b/solution.py
@@ -17,7 +17,7 @@
 SEND = 12
 BACK = 25
 CHUNKS = 2
-LIMIT = 60
+PARTS = 2
 
 
 def lane_of(shape):
@@ -28,22 +28,27 @@
     return lax.broadcasted_iota(jnp.int32, shape, 0)
 
 
-def pack_kernel(place_ref, f_hbm, k_hbm, out_ref, f_ref, k_ref, side_ref, sems):
+def pack_kernel(f_hbm, k_hbm, out_hbm, f_ref, k_ref, side_ref, out_ref, sems):
     width = BLOCKS * LANES // CHUNKS
-    copies = []
+
+    def incoming(n):
+        part = pl.ds(n * width, width)
+        pairs = ((f_hbm, f_ref), (k_hbm, k_ref))
+        return [pltpu.make_async_copy(s.at[:, part], t.at[:, part], sems.at[j, n]) for j, (s, t) in enumerate(pairs)]
+
+    def ready(n):
+        return BLOCKS if n == CHUNKS - 1 else (n + 1) * BLOCKS // CHUNKS - 2
+
+    def outgoing(n):
+        low = ready(n - 1) if n else 0
+        part = pl.ds(low * SEND, (ready(n) - low) * SEND)
+        return pltpu.make_async_copy(out_ref.at[part], out_hbm.at[part], sems.at[2, n])
+
     for n in range(CHUNKS):
-        part = pl.ds(n * width, width)
-        copies.append(
-            [
-                pltpu.make_async_copy(source.at[:, part], target.at[:, part], sems.at[j, n])
-                for j, (source, target) in enumerate(((f_hbm, f_ref), (k_hbm, k_ref)))
-            ]
-        )
-    for pair in copies:
-        for copy in pair:
+        for copy in incoming(n):
             copy.start()
 
-    step = place_ref[0]
+    step = lax.axis_index("tm").astype(jnp.int32)
     shift = lax.rem(jnp.int32(48) - 32 * step + 256, jnp.int32(128))
     first, last = step == 0, step == 4
     lane = lane_of((8, LANES))
@@ -59,11 +64,10 @@
 
     before, here, done = rolled(-1), None, 0
     for n in range(CHUNKS):
-        for copy in copies[n]:
+        for copy in incoming(n):
             copy.wait()
-        ready = BLOCKS if n == CHUNKS - 1 else (n + 1) * BLOCKS // CHUNKS - 1
         here = rolled(0) if n == 0 else here
-        for d in range(done, ready):
+        for d in range(done, ready(n)):
             after = rolled(d + 1)
             lower = jnp.where(first, before[1], here[1])
             upper = jnp.where(last, after[1], here[1])
@@ -72,14 +76,17 @@
             )
             out_ref[d * SEND : d * SEND + 8, :] = tile(f_ref, d)
             before, here = here, after
-        done = ready
-    for d in range(BLOCKS):
-        upper, lower = side_ref[8 * d : 8 * d + 4, :], side_ref[8 * d + 4 : 8 * d + 8, :]
-        folded = jnp.where(lane[:4] < 64, upper, pltpu.roll(lower, 64, 1))
-        out_ref[d * SEND + 8 : d * SEND + 12, :] = folded
-
-
-def main_kernel(place_ref, in_ref, out_ref, sides, k, s, gn, gw, r0, r1, a, b, q0, q1, q2):
+        for d in range(done, ready(n)):
+            upper, lower = side_ref[8 * d : 8 * d + 4, :], side_ref[8 * d + 4 : 8 * d + 8, :]
+            folded = jnp.where(lane[:4] < 64, upper, pltpu.roll(lower, 64, 1))
+            out_ref[d * SEND + 8 : d * SEND + 12, :] = folded
+        done = ready(n)
+        outgoing(n).start()
+    for n in range(CHUNKS):
+        outgoing(n).wait()
+
+
+def main_kernel(in_ref, out_ref, sides, k, s, gn, gw, r0, r1, a, b, q0, q1, q2):
     lane = lane_of((8, LANES))
     sub = row_of((8, LANES))
     edge = jnp.zeros((PAD, LANES), jnp.float32)
@@ -124,7 +131,8 @@
         s[at(i), :] = scale
         r0[:, at(i), :] = scale * r0[:, at(i), :]
 
-    origin = (place_ref[0] * STRIPS + place_ref[1]) * LANES - HALO
+    block = lax.axis_index("tm") * STRIPS + lax.axis_index("space")
+    origin = block.astype(jnp.int32) * LANES - HALO
 
     @pl.loop(0, TILES, unroll=True)
     def _(i):
@@ -202,7 +210,13 @@
         return (x * (0.75 * x + 0.125 * g) + 0.5 * (g * g),)
 
     (m6,) = sweep(a, *most, square, 1)
-    (m7,) = sweep(b, 2, TILES - 2, lambda i, x, g: (0.5 * (x * g),), 1)
+
+    def edges_of(i, total):
+        x = b[:, at(i), :]
+        g = gn[at(i), :] * pltpu.roll(x, 1, 2) + gw[at(i), :] * b[:, at(i, -1), :]
+        return total + jnp.sum(x * g, axis=0)
+
+    m7 = lax.fori_loop(HALO // 8, (HALO + LANES) // 8, edges_of, jnp.zeros((8, LANES), jnp.float32), unroll=True)
 
     moments = jnp.zeros((8, LANES), jnp.float32)
     for n, value in enumerate((m0, m1, m2, m3, m4, m5, m6 + m7)):
@@ -269,7 +283,7 @@
     return x[:3]
 
 
-def final_kernel(in_ref, out_ref):
+def final_kernel(in_ref, out_hbm, out_ref, sems):
     total = jnp.zeros((8, LANES), jnp.float32)
     for j in range(BLOCKS // 8):
         total = total + in_ref[pl.ds(24 + 8 * BACK * j, 8, stride=BACK), :]
@@ -277,10 +291,20 @@
     line = jnp.broadcast_to(jnp.sum(total, axis=0, keepdims=True), (8, LANES))
     m = [jnp.broadcast_to(jnp.sum(jnp.where(lane == n, line, 0.0), axis=1, keepdims=True), (8, LANES)) for n in range(7)]
     x0, x1, x2 = coefficients(m)
-    for d in range(BLOCKS):
-        at = BACK * d
-        first, second, third = in_ref[at : at + 8, :], in_ref[at + 8 : at + 16, :], in_ref[at + 16 : at + 24, :]
-        out_ref[:, d * LANES : (d + 1) * LANES] = x0 * first + x1 * second + x2 * third
+    width = BLOCKS // PARTS
+
+    def outgoing(n):
+        part = pl.ds(n * width * LANES, width * LANES)
+        return pltpu.make_async_copy(out_ref.at[:, part], out_hbm.at[:, part], sems.at[n])
+
+    for n in range(PARTS):
+        for d in range(n * width, (n + 1) * width):
+            at = BACK * d
+            first, second, third = in_ref[at : at + 8, :], in_ref[at + 8 : at + 16, :], in_ref[at + 16 : at + 24, :]
+            out_ref[:, d * LANES : (d + 1) * LANES] = x0 * first + x1 * second + x2 * third
+        outgoing(n).start()
+    for n in range(PARTS):
+        outgoing(n).wait()
 
 
 def exchanged(blocks, rows):
@@ -291,40 +315,40 @@
 
 def body(forcing, conductivity):
     columns = forcing.shape[2]
-    place = jnp.stack([lax.axis_index("tm"), lax.axis_index("space")]).astype(jnp.int32)
-    scalar, whole = pl.BlockSpec(memory_space=pltpu.SMEM), pl.BlockSpec(memory_space=pltpu.VMEM)
-    held = pl.BlockSpec(memory_space=pl.ANY)
-    params = pltpu.CompilerParams(vmem_limit_bytes=40 * 2**20)
+    whole, held = pl.BlockSpec(memory_space=pltpu.VMEM), pl.BlockSpec(memory_space=pl.ANY)
+    strip = pltpu.VMEM((8, columns), jnp.float32)
     packed = pl.pallas_call(
         pack_kernel,
         out_shape=jax.ShapeDtypeStruct((BLOCKS * SEND, LANES), jnp.float32),
-        in_specs=[scalar, held, held],
-        out_specs=whole,
+        in_specs=[held, held],
+        out_specs=held,
         scratch_shapes=[
-            pltpu.VMEM((8, columns), jnp.float32),
-            pltpu.VMEM((8, columns), jnp.float32),
+            strip,
+            strip,
             pltpu.VMEM((BLOCKS * 8, LANES), jnp.float32),
-            pltpu.SemaphoreType.DMA((2, CHUNKS)),
+            pltpu.VMEM((BLOCKS * SEND, LANES), jnp.float32),
+            pltpu.SemaphoreType.DMA((3, CHUNKS)),
         ],
-        compiler_params=pltpu.CompilerParams(vmem_limit_bytes=LIMIT * 2**20),
+        compiler_params=pltpu.CompilerParams(vmem_limit_bytes=60 * 2**20),
         name="pack",
-    )(place, forcing.reshape(8, columns), conductivity)
+    )(forcing.reshape(8, columns), conductivity)
     flat, field = pltpu.VMEM((TALL, LANES), jnp.float32), pltpu.VMEM((STEPS, TALL, LANES), jnp.float32)
     basis = pl.pallas_call(
         main_kernel,
         out_shape=jax.ShapeDtypeStruct((BLOCKS * BACK, LANES), jnp.float32),
-        in_specs=[scalar, whole],
+        in_specs=[whole],
         out_specs=whole,
         scratch_shapes=[pltpu.VMEM((LANES, LANES), jnp.float32)] + [flat] * 4 + [field] * 7,
-        compiler_params=params,
+        compiler_params=pltpu.CompilerParams(vmem_limit_bytes=40 * 2**20),
         name="basis",
-    )(place, exchanged(packed, SEND))
+    )(exchanged(packed, SEND))
     out = pl.pallas_call(
         final_kernel,
         out_shape=jax.ShapeDtypeStruct((8, columns), jnp.float32),
         in_specs=[whole],
-        out_specs=whole,
-        compiler_params=params,
+        out_specs=held,
+        scratch_shapes=[strip, pltpu.SemaphoreType.DMA((PARTS,))],
+        compiler_params=pltpu.CompilerParams(vmem_limit_bytes=40 * 2**20),
         name="combine",
     )(exchanged(basis, BACK))
     return out.reshape(1, 8, columns)

time: 69.1 us -> 66.9 us (0.968)
  Pallas kernels: 10.7 us -> 9.09 us
    pallas_call x1, Pallas kernels: 3.3 us -> 2.42 us  [body(): pl.pallas_call(pack_kernel, out_shape=jax.ShapeDtypeStruct((BLOCKS * SEND...]
    pallas_call x1, Pallas kernels: 6.28 us -> 5.59 us  [body(): pl.pallas_call(main_kernel, out_shape=jax.ShapeDtypeStruct((BLOCKS * BACK...]
where the time goes in v4:
time: 66.9 us; the launch traced here: 66.8 us
  blocking collectives  57.6 us (86%)
  Pallas kernels  9.09 us (14%)
    all_to_all x2, blocking collectives, exchanged(): moved = lax.all_to_all(pieces, ('tm', 'space'), split_axis=0, concat_axis=0)  57.6 us
    pallas_call x1, Pallas kernels, body(): pl.pallas_call(main_kernel, out_shape=jax.ShapeDtypeStruct((BLOCKS * BACK...  5.59 us
    pallas_call x1, Pallas kernels, body(): pl.pallas_call(pack_kernel, out_shape=jax.ShapeDtypeStruct((BLOCKS * SEND...  2.42 us

profile of v4, /device:TPU:1, one launch (start us, length us, event | category | flops | bytes accessed | tf_op | source)
XLA Modules:
  0.0 66.8 jit_solution(7211213339245019094)
XLA Ops:
  0.0 2.4 %pack.1 = f32[1536,128]{1,0:T(8,128)} custom-call(f32[8,16384]{1,0:T(8,128)} %bitcast.10, f32[8,16384]{1,0:T(8,128)} %k_hbm.1), custom_call_target="tpu_custom_call" | custom-call | tf_op jit(solution)/shard_map/pack/pallas_call | solution.py:320
  2.4 27.8 %all_to_all.10 = f32[128,12,1,128]{3,2,1,0:T(1,128)S(1)} all-to-all(f32[128,12,1,128]{3,2,1,0:T(1,128)} %bitcast.9), channel_id=1, replica_groups=mesh['tm'=8,'space'=16] {'tm','space'}, dimensions={0} | all-to-all | bytes 1572864 | tf_op jit(solution)/shard_map/all_to_all | solution.py:312
  30.2 5.6 %basis.1 = f32[3200,128]{1,0:T(8,128)S(1)} custom-call(f32[1536,128]{1,0:T(8,128)S(1)} %bitcast.8), custom_call_target="tpu_custom_call" | custom-call | tf_op jit(solution)/shard_map/basis/pallas_call | solution.py:336
  35.8 29.9 %all_to_all.11 = f32[128,25,1,128]{3,2,1,0:T(1,128)S(1)} all-to-all(f32[128,25,1,128]{3,2,1,0:T(1,128)S(1)} %bitcast.6), channel_id=1, replica_groups=mesh['tm'=8,'space'=16] {'tm','space'}, dimensions={0} | all-to-all | bytes 3276800 | tf_op jit(solution)/shard_map/all_to_all | solution.py:312
  65.7 1.1 %combine.1 = f32[8,16384]{1,0:T(8,128)} custom-call(f32[3200,128]{1,0:T(8,128)S(1)} %bitcast.7), custom_call_target="tpu_custom_call" | custom-call | tf_op jit(solution)/shard_map/combine/pallas_call | solution.py:345

commit v5 on v4

--- a/solution.py
+++ b/solution.py
@@ -14,7 +14,7 @@
 PAD = 8
 TALL = WIDE + 2 * PAD
 TILES = WIDE // 8
-SEND = 12
+SEND = 11
 BACK = 25
 CHUNKS = 2
 PARTS = 2
@@ -29,28 +29,26 @@
 
 
 def pack_kernel(f_hbm, k_hbm, out_hbm, f_ref, k_ref, side_ref, out_ref, sems):
+    step = lax.axis_index("tm").astype(jnp.int32)
+    row = pltpu.make_async_copy(k_hbm.at[pl.ds(step, 1), :], k_ref, sems.at[2, 0])
     width = BLOCKS * LANES // CHUNKS
 
     def incoming(n):
         part = pl.ds(n * width, width)
-        pairs = ((f_hbm, f_ref), (k_hbm, k_ref))
-        return [pltpu.make_async_copy(s.at[:, part], t.at[:, part], sems.at[j, n]) for j, (s, t) in enumerate(pairs)]
+        return pltpu.make_async_copy(f_hbm.at[:, part], f_ref.at[:, part], sems.at[0, n])
 
     def ready(n):
-        return BLOCKS if n == CHUNKS - 1 else (n + 1) * BLOCKS // CHUNKS - 2
+        return BLOCKS if n == CHUNKS - 1 else (n + 1) * BLOCKS // CHUNKS - 8
 
     def outgoing(n):
         low = ready(n - 1) if n else 0
         part = pl.ds(low * SEND, (ready(n) - low) * SEND)
-        return pltpu.make_async_copy(out_ref.at[part], out_hbm.at[part], sems.at[2, n])
-
+        return pltpu.make_async_copy(out_ref.at[part], out_hbm.at[part], sems.at[1, n])
+
+    row.start()
     for n in range(CHUNKS):
-        for copy in incoming(n):
-            copy.start()
-
-    step = lax.axis_index("tm").astype(jnp.int32)
-    shift = lax.rem(jnp.int32(48) - 32 * step + 256, jnp.int32(128))
-    first, last = step == 0, step == 4
+        incoming(n).start()
+
     lane = lane_of((8, LANES))
     zero = jnp.zeros((8, LANES), jnp.float32)
 
@@ -59,27 +57,34 @@
 
     def rolled(d):
         if d < 0 or d >= BLOCKS:
-            return zero, zero
-        return pltpu.roll(tile(f_ref, d), 16, 1), pltpu.roll(tile(k_ref, d), shift, 1)
-
+            return zero
+        return pltpu.roll(tile(f_ref, d), 14, 1)
+
+    def spread(d):
+        if d < 0 or d >= BLOCKS:
+            return zero
+        return jnp.broadcast_to(tile(k_ref, d), (8, LANES))
+
+    row.wait()
     before, here, done = rolled(-1), None, 0
     for n in range(CHUNKS):
-        for copy in incoming(n):
-            copy.wait()
+        incoming(n).wait()
         here = rolled(0) if n == 0 else here
         for d in range(done, ready(n)):
             after = rolled(d + 1)
-            lower = jnp.where(first, before[1], here[1])
-            upper = jnp.where(last, after[1], here[1])
-            side_ref[8 * d : 8 * d + 8, :] = jnp.where(
-                lane < 16, before[0], jnp.where(lane < 32, after[0], jnp.where(lane < 48, lower, upper))
-            )
+            beside = jnp.where(lane >= 64, spread(d - 1), spread(d + 1))
+            beside = pltpu.roll(beside, 16, 1, stride=4, stride_axis=0)
+            side_ref[8 * d : 8 * d + 8, :] = jnp.where(lane < 14, before, jnp.where(lane < 28, after, beside))
             out_ref[d * SEND : d * SEND + 8, :] = tile(f_ref, d)
+            out_ref[d * SEND + 10 : d * SEND + 11, :] = tile(k_ref, d)
             before, here = here, after
-        for d in range(done, ready(n)):
-            upper, lower = side_ref[8 * d : 8 * d + 4, :], side_ref[8 * d + 4 : 8 * d + 8, :]
-            folded = jnp.where(lane[:4] < 64, upper, pltpu.roll(lower, 64, 1))
-            out_ref[d * SEND + 8 : d * SEND + 12, :] = folded
+        for d in range(done, ready(n), 4):
+            group = [side_ref[pl.ds(8 * d + q, 8, stride=4), :] for q in range(4)]
+            group = [group[0]] + [pltpu.roll(group[q], 32 * q, 1) for q in range(1, 4)]
+            folded = jnp.where(lane < 64, jnp.where(lane < 32, *group[:2]), jnp.where(lane < 96, *group[2:]))
+            for m in range(4):
+                at = (d + m) * SEND + 8
+                out_ref[at : at + 2, :] = folded[2 * m : 2 * m + 2]
         done = ready(n)
         outgoing(n).start()
     for n in range(CHUNKS):
@@ -98,20 +103,32 @@
         ref[:, 0:PAD, :] = edges
         ref[:, PAD + WIDE : TALL, :] = edges
 
+    for rows in (slice(PAD, PAD + 2), slice(PAD + WIDE - 2, PAD + WIDE)):
+        r0[:, rows, :] = jnp.zeros((STEPS, 2, LANES), jnp.float32)
+    own = slice(PAD + HALO, PAD + HALO + LANES)
+    beside = []
     for t in range(STEPS):
-        rows = []
-        for i in range(STRIPS):
-            at = SEND * (STRIPS * t + i)
-            rows.append(in_ref[at : at + 8, :])
-            piece = in_ref[at + 8 : at + 12, :]
-            sides[8 * i : 8 * i + 4, :] = piece
-            sides[8 * i + 4 : 8 * i + 8, :] = pltpu.roll(piece, 64, 1)
-        r0[t, PAD + HALO : PAD + HALO + LANES, :] = jnp.concatenate(rows, 0).T
+        base = SEND * STRIPS * t
+        rows = [in_ref[base + SEND * i : base + SEND * i + 8, :] for i in range(STRIPS)]
+        r0[t, own, :] = jnp.concatenate(rows, 0).T
+        for j in range(2):
+            groups = in_ref[pl.ds(base + 8 + j, STRIPS, stride=SEND), :]
+            for q in range(4):
+                sides[pl.ds(4 * j + q, STRIPS, stride=8), :] = pltpu.roll(groups, LANES - 32 * q, 1) if q else groups
         turned = sides[...].T
-        r0[t, PAD : PAD + HALO, :] = turned[0:16]
-        r0[t, PAD + HALO + LANES : PAD + WIDE, :] = turned[16:32]
-        if t < 5:
-            k[PAD + 32 * t : PAD + 32 * t + 32, :] = turned[32:64]
+        r0[t, PAD + 2 : PAD + HALO, :] = turned[0:14]
+        r0[t, PAD + HALO + LANES : PAD + WIDE - 2, :] = turned[14:28]
+        beside.append(turned[28:32])
+    rows = [in_ref[pl.ds(SEND * i + 10, 8, stride=SEND * STRIPS), :] for i in range(STRIPS)]
+    k[own, :] = jnp.concatenate(rows, 0).T
+    for r in range(8):
+        made = jnp.zeros((4, LANES), jnp.float32)
+        for t in range(STEPS):
+            moved = beside[t] if t == r else pltpu.roll(beside[t], (t - r) % LANES, 1)
+            made = jnp.where(lane[:4] % 8 == t, moved, made)
+        v = 4 * (7 - r)
+        to = PAD + v if v < HALO else PAD + LANES + v
+        k[to : to + 4, :] = made
 
     def at(i, offset=0):
         return pl.ds(pl.multiple_of(8 * i + PAD, 8) + offset, 8)
@@ -224,7 +241,6 @@
     totals = jnp.sum(moments, axis=1, keepdims=True)
     line = jnp.sum(jnp.where(lane == sub, totals, 0.0), axis=0, keepdims=True)
 
-    own = slice(PAD + HALO, PAD + HALO + LANES)
     for t in range(STEPS):
         for field, (ref, step) in enumerate(((q0, STEPS - 1 - t), (q1, t), (q2, STEPS - 1 - t))):
             turned = (s[own, :] * ref[step, own, :]).T
@@ -324,7 +340,7 @@
         out_specs=held,
         scratch_shapes=[
             strip,
-            strip,
+            pltpu.VMEM((1, columns), jnp.float32),
             pltpu.VMEM((BLOCKS * 8, LANES), jnp.float32),
             pltpu.VMEM((BLOCKS * SEND, LANES), jnp.float32),
             pltpu.SemaphoreType.DMA((3, CHUNKS)),

time: 66.9 us -> 66.2 us (0.990)
    all_to_all x2, blocking collectives: 57.6 us -> 57 us  [exchanged(): moved = lax.all_to_all(pieces, ('tm', 'space'), split_axis=0, concat_axis=0)]
where the time goes in v5:
time: 66.2 us; the launch traced here: 66 us
  blocking collectives  57 us (86%)
  Pallas kernels  9.08 us (14%)
    all_to_all x2, blocking collectives, exchanged(): moved = lax.all_to_all(pieces, ('tm', 'space'), split_axis=0, concat_axis=0)  57 us
    pallas_call x1, Pallas kernels, body(): pl.pallas_call(main_kernel, out_shape=jax.ShapeDtypeStruct((BLOCKS * BACK...  5.61 us
    pallas_call x1, Pallas kernels, body(): pl.pallas_call(pack_kernel, out_shape=jax.ShapeDtypeStruct((BLOCKS * SEND...  2.38 us

profile of v5, /device:TPU:1, one launch (start us, length us, event | category | flops | bytes accessed | tf_op | source)
XLA Modules:
  0.0 66.0 jit_solution(4452077686179079903)
XLA Ops:
  0.0 2.4 %pack.1 = f32[1408,128]{1,0:T(8,128)} custom-call(f32[8,16384]{1,0:T(8,128)} %bitcast.10, f32[8,16384]{1,0:T(8,128)} %k_hbm.1), custom_call_target="tpu_custom_call" | custom-call | tf_op jit(solution)/shard_map/pack/pallas_call | solution.py:336
  2.4 27.1 %all_to_all.10 = f32[128,11,1,128]{3,2,1,0:T(1,128)S(1)} all-to-all(f32[128,11,1,128]{3,2,1,0:T(1,128)} %bitcast.9), channel_id=1, replica_groups=mesh['tm'=8,'space'=16] {'tm','space'}, dimensions={0} | all-to-all | bytes 1441792 | tf_op jit(solution)/shard_map/all_to_all | solution.py:328
  29.4 5.6 %basis.1 = f32[3200,128]{1,0:T(8,128)S(1)} custom-call(f32[1408,128]{1,0:T(8,128)S(1)} %bitcast.8), custom_call_target="tpu_custom_call" | custom-call | tf_op jit(solution)/shard_map/basis/pallas_call | solution.py:352
  35.1 29.9 %all_to_all.11 = f32[128,25,1,128]{3,2,1,0:T(1,128)S(1)} all-to-all(f32[128,25,1,128]{3,2,1,0:T(1,128)S(1)} %bitcast.6), channel_id=1, replica_groups=mesh['tm'=8,'space'=16] {'tm','space'}, dimensions={0} | all-to-all | bytes 3276800 | tf_op jit(solution)/shard_map/all_to_all | solution.py:328
  65.0 1.1 %combine.1 = f32[8,16384]{1,0:T(8,128)} custom-call(f32[3200,128]{1,0:T(8,128)S(1)} %bitcast.7), custom_call_target="tpu_custom_call" | custom-call | tf_op jit(solution)/shard_map/combine/pallas_call | solution.py:361

commit v6 on v5

--- a/solution.py
+++ b/solution.py
@@ -28,22 +28,17 @@
     return lax.broadcasted_iota(jnp.int32, shape, 0)
 
 
-def pack_kernel(f_hbm, k_hbm, out_hbm, f_ref, k_ref, side_ref, out_ref, sems):
+def pack_kernel(f_hbm, k_hbm, out_ref, f_ref, k_ref, side_ref, sems):
     step = lax.axis_index("tm").astype(jnp.int32)
-    row = pltpu.make_async_copy(k_hbm.at[pl.ds(step, 1), :], k_ref, sems.at[2, 0])
+    row = pltpu.make_async_copy(k_hbm.at[pl.ds(step, 1), :], k_ref, sems.at[CHUNKS])
     width = BLOCKS * LANES // CHUNKS
 
     def incoming(n):
         part = pl.ds(n * width, width)
-        return pltpu.make_async_copy(f_hbm.at[:, part], f_ref.at[:, part], sems.at[0, n])
+        return pltpu.make_async_copy(f_hbm.at[:, part], f_ref.at[:, part], sems.at[n])
 
     def ready(n):
         return BLOCKS if n == CHUNKS - 1 else (n + 1) * BLOCKS // CHUNKS - 8
-
-    def outgoing(n):
-        low = ready(n - 1) if n else 0
-        part = pl.ds(low * SEND, (ready(n) - low) * SEND)
-        return pltpu.make_async_copy(out_ref.at[part], out_hbm.at[part], sems.at[1, n])
 
     row.start()
     for n in range(CHUNKS):
@@ -86,9 +81,6 @@
                 at = (d + m) * SEND + 8
                 out_ref[at : at + 2, :] = folded[2 * m : 2 * m + 2]
         done = ready(n)
-        outgoing(n).start()
-    for n in range(CHUNKS):
-        outgoing(n).wait()
 
 
 def main_kernel(in_ref, out_ref, sides, k, s, gn, gw, r0, r1, a, b, q0, q1, q2):
@@ -329,25 +321,28 @@
     return moved.reshape(-1).reshape(BLOCKS * rows, LANES)
 
 
+def in_hbm(array):
+    return pltpu.with_memory_space_constraint(array, pltpu.HBM)
+
+
 def body(forcing, conductivity):
     columns = forcing.shape[2]
     whole, held = pl.BlockSpec(memory_space=pltpu.VMEM), pl.BlockSpec(memory_space=pl.ANY)
     strip = pltpu.VMEM((8, columns), jnp.float32)
     packed = pl.pallas_call(
         pack_kernel,
-        out_shape=jax.ShapeDtypeStruct((BLOCKS * SEND, LANES), jnp.float32),
+        out_shape=pltpu.VMEM((BLOCKS * SEND, LANES), jnp.float32),
         in_specs=[held, held],
-        out_specs=held,
+        out_specs=whole,
         scratch_shapes=[
             strip,
             pltpu.VMEM((1, columns), jnp.float32),
             pltpu.VMEM((BLOCKS * 8, LANES), jnp.float32),
-            pltpu.VMEM((BLOCKS * SEND, LANES), jnp.float32),
-            pltpu.SemaphoreType.DMA((3, CHUNKS)),
+            pltpu.SemaphoreType.DMA((CHUNKS + 1,)),
         ],
-        compiler_params=pltpu.CompilerParams(vmem_limit_bytes=60 * 2**20),
+        compiler_params=pltpu.CompilerParams(vmem_limit_bytes=40 * 2**20),
         name="pack",
-    )(forcing.reshape(8, columns), conductivity)
+    )(in_hbm(forcing.reshape(8, columns)), in_hbm(conductivity))
     flat, field = pltpu.VMEM((TALL, LANES), jnp.float32), pltpu.VMEM((STEPS, TALL, LANES), jnp.float32)
     basis = pl.pallas_call(
         main_kernel,

time: 66.2 us -> 65.3 us (0.986)
  Pallas kernels: 9.08 us -> 8.36 us
    pallas_call x1, Pallas kernels: 2.38 us -> 1.66 us  [body(): pl.pallas_call(pack_kernel, out_shape=pltpu.VMEM((BLOCKS * SEND, LANES),...]
where the time goes in v6:
time: 65.3 us; the launch traced here: 65.1 us
  blocking collectives  56.7 us (87%)
  Pallas kernels  8.36 us (13%)
    all_to_all x2, blocking collectives, exchanged(): moved = lax.all_to_all(pieces, ('tm', 'space'), split_axis=0, concat_axis=0)  56.7 us
    pallas_call x1, Pallas kernels, body(): pl.pallas_call(main_kernel, out_shape=jax.ShapeDtypeStruct((BLOCKS * BACK...  5.61 us
    pallas_call x1, Pallas kernels, body(): pl.pallas_call(pack_kernel, out_shape=pltpu.VMEM((BLOCKS * SEND, LANES),...  1.66 us

profile of v6, /device:TPU:1, one launch (start us, length us, event | category | flops | bytes accessed | tf_op | source)
XLA Modules:
  0.0 65.1 jit_solution(989951109065997181)
XLA Ops:
  0.0 1.7 %pack.1 = f32[1408,128]{1,0:T(8,128)S(1)} custom-call(f32[8,16384]{1,0:T(8,128)} %bitcast.10, f32[8,16384]{1,0:T(8,128)} %k_hbm.1), custom_call_target="tpu_custom_call" | custom-call | tf_op jit(solution)/shard_map/pack/pallas_call | solution.py:332
  1.7 26.8 %all_to_all.10 = f32[128,11,1,128]{3,2,1,0:T(1,128)S(1)} all-to-all(f32[128,11,1,128]{3,2,1,0:T(1,128)S(1)} %bitcast.8), channel_id=1, replica_groups=mesh['tm'=8,'space'=16] {'tm','space'}, dimensions={0} | all-to-all | bytes 1441792 | tf_op jit(solution)/shard_map/all_to_all | solution.py:320
  28.5 5.6 %basis.1 = f32[3200,128]{1,0:T(8,128)S(1)} custom-call(f32[1408,128]{1,0:T(8,128)S(1)} %bitcast.9), custom_call_target="tpu_custom_call" | custom-call | tf_op jit(solution)/shard_map/basis/pallas_call | solution.py:347
  34.1 29.9 %all_to_all.11 = f32[128,25,1,128]{3,2,1,0:T(1,128)S(1)} all-to-all(f32[128,25,1,128]{3,2,1,0:T(1,128)S(1)} %bitcast.6), channel_id=1, replica_groups=mesh['tm'=8,'space'=16] {'tm','space'}, dimensions={0} | all-to-all | bytes 3276800 | tf_op jit(solution)/shard_map/all_to_all | solution.py:320
  64.0 1.1 %combine.1 = f32[8,16384]{1,0:T(8,128)} custom-call(f32[3200,128]{1,0:T(8,128)S(1)} %bitcast.7), custom_call_target="tpu_custom_call" | custom-call | tf_op jit(solution)/shard_map/combine/pallas_call | solution.py:356

commit v7 on v6

--- a/solution.py
+++ b/solution.py
@@ -16,7 +16,7 @@
 TILES = WIDE // 8
 SEND = 11
 BACK = 25
-CHUNKS = 2
+CHUNKS = 1
 PARTS = 2
 
 
@@ -99,18 +99,23 @@
         r0[:, rows, :] = jnp.zeros((STEPS, 2, LANES), jnp.float32)
     own = slice(PAD + HALO, PAD + HALO + LANES)
     beside = []
-    for t in range(STEPS):
-        base = SEND * STRIPS * t
-        rows = [in_ref[base + SEND * i : base + SEND * i + 8, :] for i in range(STRIPS)]
-        r0[t, own, :] = jnp.concatenate(rows, 0).T
+    wide = lane_of((STRIPS, LANES))
+    for low in range(0, STEPS, 4):
+        for t in range(low, low + 4):
+            base = SEND * STRIPS * t
+            rows = [in_ref[base + SEND * i : base + SEND * i + 8, :] for i in range(STRIPS)]
+            r0[t, own, :] = jnp.concatenate(rows, 0).T
         for j in range(2):
-            groups = in_ref[pl.ds(base + 8 + j, STRIPS, stride=SEND), :]
+            packed = [in_ref[pl.ds(SEND * STRIPS * (low + m) + 8 + j, STRIPS, stride=SEND), :] for m in range(4)]
             for q in range(4):
-                sides[pl.ds(4 * j + q, STRIPS, stride=8), :] = pltpu.roll(groups, LANES - 32 * q, 1) if q else groups
+                moved = [v if m == q else pltpu.roll(v, 32 * (m - q) % LANES, 1) for m, v in enumerate(packed)]
+                joined = jnp.where(wide < 64, jnp.where(wide < 32, *moved[:2]), jnp.where(wide < 96, *moved[2:]))
+                sides[pl.ds(4 * j + q, STRIPS, stride=8), :] = joined
         turned = sides[...].T
-        r0[t, PAD + 2 : PAD + HALO, :] = turned[0:14]
-        r0[t, PAD + HALO + LANES : PAD + WIDE - 2, :] = turned[14:28]
-        beside.append(turned[28:32])
+        for m in range(4):
+            r0[low + m, PAD + 2 : PAD + HALO, :] = turned[32 * m : 32 * m + 14]
+            r0[low + m, PAD + HALO + LANES : PAD + WIDE - 2, :] = turned[32 * m + 14 : 32 * m + 28]
+            beside.append(turned[32 * m + 28 : 32 * m + 32])
     rows = [in_ref[pl.ds(SEND * i + 10, 8, stride=SEND * STRIPS), :] for i in range(STRIPS)]
     k[own, :] = jnp.concatenate(rows, 0).T
     for r in range(8):

time: 65.3 us -> 65.1 us (level)
  no operation moved by 1% of the time
where the time goes in v7:
time: 65.1 us; the launch traced here: 64.9 us
  blocking collectives  56.7 us (87%)
  Pallas kernels  8.18 us (13%)
    all_to_all x2, blocking collectives, exchanged(): moved = lax.all_to_all(pieces, ('tm', 'space'), split_axis=0, concat_axis=0)  56.7 us
    pallas_call x1, Pallas kernels, body(): pl.pallas_call(main_kernel, out_shape=jax.ShapeDtypeStruct((BLOCKS * BACK...  5.5 us
    pallas_call x1, Pallas kernels, body(): pl.pallas_call(pack_kernel, out_shape=pltpu.VMEM((BLOCKS * SEND, LANES),...  1.6 us

profile of v7, /device:TPU:1, one launch (start us, length us, event | category | flops | bytes accessed | tf_op | source)
XLA Modules:
  0.0 64.9 jit_solution(15614875744726787311)
XLA Ops:
  0.0 1.6 %pack.1 = f32[1408,128]{1,0:T(8,128)S(1)} custom-call(f32[8,16384]{1,0:T(8,128)} %bitcast.10, f32[8,16384]{1,0:T(8,128)} %k_hbm.1), custom_call_target="tpu_custom_call" | custom-call | tf_op jit(solution)/shard_map/pack/pallas_call | solution.py:337
  1.6 26.8 %all_to_all.10 = f32[128,11,1,128]{3,2,1,0:T(1,128)S(1)} all-to-all(f32[128,11,1,128]{3,2,1,0:T(1,128)S(1)} %bitcast.8), channel_id=1, replica_groups=mesh['tm'=8,'space'=16] {'tm','space'}, dimensions={0} | all-to-all | bytes 1441792 | tf_op jit(solution)/shard_map/all_to_all | solution.py:325
  28.5 5.5 %basis.1 = f32[3200,128]{1,0:T(8,128)S(1)} custom-call(f32[1408,128]{1,0:T(8,128)S(1)} %bitcast.9), custom_call_target="tpu_custom_call" | custom-call | tf_op jit(solution)/shard_map/basis/pallas_call | solution.py:352
  34.0 29.9 %all_to_all.11 = f32[128,25,1,128]{3,2,1,0:T(1,128)S(1)} all-to-all(f32[128,25,1,128]{3,2,1,0:T(1,128)S(1)} %bitcast.6), channel_id=1, replica_groups=mesh['tm'=8,'space'=16] {'tm','space'}, dimensions={0} | all-to-all | bytes 3276800 | tf_op jit(solution)/shard_map/all_to_all | solution.py:325
  63.9 1.1 %combine.1 = f32[8,16384]{1,0:T(8,128)} custom-call(f32[3200,128]{1,0:T(8,128)S(1)} %bitcast.7), custom_call_target="tpu_custom_call" | custom-call | tf_op jit(solution)/shard_map/combine/pallas_call | solution.py:361

commit v8 on v7

--- a/solution.py
+++ b/solution.py
@@ -209,10 +209,19 @@
     def mirrored(x, r):
         return (r * turned_in_time(x),)
 
+    def send(field, ref, mirror):
+        for t in range(STEPS):
+            turned = (s[own, :] * ref[STEPS - 1 - t if mirror else t, own, :]).T
+            for i in range(STRIPS):
+                to = BACK * (STRIPS * t + i) + 8 * field
+                out_ref[to : to + 8, :] = turned[8 * i : 8 * i + 8]
+
     full, most = (0, TILES), (1, TILES - 1)
     (m0,) = polynomial(r0, q0, (full, full, full), same, 1)
+    send(0, q0, True)
     (m1,) = operate(q0, r1, full, True, mirrored, 1)
     (m2,) = polynomial(r1, q1, (full, most, most), same, 1)
+    send(1, q1, False)
     operate(q1, r0, most, False, lambda x, r: (), 0)
     m4, m3 = polynomial(
         r0, q2, (most, most, most), lambda i, v, q: (v * q, r1[:, at(i), :] * turned_in_time(q)), 2
@@ -238,12 +247,7 @@
     totals = jnp.sum(moments, axis=1, keepdims=True)
     line = jnp.sum(jnp.where(lane == sub, totals, 0.0), axis=0, keepdims=True)
 
-    for t in range(STEPS):
-        for field, (ref, step) in enumerate(((q0, STEPS - 1 - t), (q1, t), (q2, STEPS - 1 - t))):
-            turned = (s[own, :] * ref[step, own, :]).T
-            for i in range(STRIPS):
-                to = BACK * (STRIPS * t + i) + 8 * field
-                out_ref[to : to + 8, :] = turned[8 * i : 8 * i + 8]
+    send(2, q2, True)
     for d in range(BLOCKS):
         out_ref[BACK * d + 24 : BACK * d + 25, :] = line
 

time: 65.1 us -> 65.1 us (level)
  no operation moved by 1% of the time
where the time goes in v8:
time: 65.1 us; the launch traced here: 64.9 us
  blocking collectives  56.7 us (87%)
  Pallas kernels  8.18 us (13%)
    all_to_all x2, blocking collectives, exchanged(): moved = lax.all_to_all(pieces, ('tm', 'space'), split_axis=0, concat_axis=0)  56.7 us
    pallas_call x1, Pallas kernels, body(): pl.pallas_call(main_kernel, out_shape=jax.ShapeDtypeStruct((BLOCKS * BACK...  5.5 us
    pallas_call x1, Pallas kernels, body(): pl.pallas_call(pack_kernel, out_shape=pltpu.VMEM((BLOCKS * SEND, LANES),...  1.6 us

profile of v8, /device:TPU:1, one launch (start us, length us, event | category | flops | bytes accessed | tf_op | source)
XLA Modules:
  0.0 64.9 jit_solution(10416668738854962914)
XLA Ops:
  0.0 1.6 %pack.1 = f32[1408,128]{1,0:T(8,128)S(1)} custom-call(f32[8,16384]{1,0:T(8,128)} %bitcast.10, f32[8,16384]{1,0:T(8,128)} %k_hbm.1), custom_call_target="tpu_custom_call" | custom-call | tf_op jit(solution)/shard_map/pack/pallas_call | solution.py:341
  1.6 26.8 %all_to_all.10 = f32[128,11,1,128]{3,2,1,0:T(1,128)S(1)} all-to-all(f32[128,11,1,128]{3,2,1,0:T(1,128)S(1)} %bitcast.8), channel_id=1, replica_groups=mesh['tm'=8,'space'=16] {'tm','space'}, dimensions={0} | all-to-all | bytes 1441792 | tf_op jit(solution)/shard_map/all_to_all | solution.py:329
  28.5 5.5 %basis.1 = f32[3200,128]{1,0:T(8,128)S(1)} custom-call(f32[1408,128]{1,0:T(8,128)S(1)} %bitcast.9), custom_call_target="tpu_custom_call" | custom-call | tf_op jit(solution)/shard_map/basis/pallas_call | solution.py:356
  34.0 29.9 %all_to_all.11 = f32[128,25,1,128]{3,2,1,0:T(1,128)S(1)} all-to-all(f32[128,25,1,128]{3,2,1,0:T(1,128)S(1)} %bitcast.6), channel_id=1, replica_groups=mesh['tm'=8,'space'=16] {'tm','space'}, dimensions={0} | all-to-all | bytes 3276800 | tf_op jit(solution)/shard_map/all_to_all | solution.py:329
  63.9 1.1 %combine.1 = f32[8,16384]{1,0:T(8,128)} custom-call(f32[3200,128]{1,0:T(8,128)S(1)} %bitcast.7), custom_call_target="tpu_custom_call" | custom-call | tf_op jit(solution)/shard_map/combine/pallas_call | solution.py:365
